TPU v7x, 32 devices: a whole 2x2x4 slice. The times are simulated.
32 devices in a mesh: group: 4 (over x, core), dp: 2 (over y), tensor: 4 (over z).
Axes of the slice: x: 2, y: 2, z: 4, core: 2. Of those that a mesh axis runs over, the one named last changes fastest.
Arguments:
- activations: bfloat16 [6144, 5120], P(('group', 'dp'), 'tensor'), may hold values from -6 to 6
- norm_gain: float32 [5120], replicated, may hold values from 0.5 to 1.5
- master_weight: float32 [5120, 4, 3, 128], P(('group', 'dp'), 'tensor'), may hold values from -0.078125 to 0.078125
- grad: bfloat16 [5120, 4, 3, 128], P(('group', 'dp'), 'tensor'), may hold values from -12 to 12
- moment: float32 [5120, 4, 3, 128], P(('group', 'dp'), 'tensor'), may hold values from -0.0048828125 to 0.0048828125
- variance: float32 [5120, 4, 3, 128], P(('group', 'dp'), 'tensor'), may hold values from 6.357829e-09 to 2.5431316e-07
- query_gain: float32 [8, 128], P('tensor'), may hold values from 1 to 2.5
- key_gain: float32 [2, 128], replicated, may hold values from 1 to 2.5
- prompt_len: int32 [8], P(('group', 'dp')), may hold values from 192 to 768, as said below
Outputs:
- attended: bfloat16 [6144, 1024], P(('group', 'dp'), 'tensor')
Inputs may be any that keep to these rules, and one draw needn't show every extreme that they name: `prompt_len`: some sequence is full.
All inputs are finite; a program needn't handle non-finite values.
Results may differ from a plain program's by a relative error of at most 0.012.
The roundings to bfloat16 on the way count: a program that leaves them out, or rounds other values in their place, can miss the bound.
Values may be sent and summed in bfloat16 or wider, within the bound.
A program may use at most 64 MiB of HBM per device.

v0:
```python
import jax
import jax.numpy as jnp
from jax import lax
from jax.sharding import PartitionSpec as P

STEP_SCALE = 0.5
BETA_ONE = 0.9
BETA_TWO = 0.95
ROPE_BASE = 500000.0


def from_partner(array, axis, distance):
    return lax.ppermute(array, axis, [(i, i ^ 1 << distance) for i in range(lax.axis_size(axis))])


def rope_tables(length, head_size):
    positions = jnp.arange(length, dtype=jnp.float32)
    exponent = jnp.arange(head_size // 2, dtype=jnp.float32) * 2.0 / head_size
    inverse = jnp.power(ROPE_BASE, -exponent)
    angles = positions[:, None] * inverse[None, :]
    return (jnp.cos(angles), jnp.sin(angles))


def rotate(inputs, cosine, sine):
    midpoint = inputs.shape[-1] // 2
    front_half = inputs[..., :midpoint]
    back_half = inputs[..., midpoint:]
    return jnp.concatenate(
        [front_half * cosine - back_half * sine, back_half * cosine + front_half * sine], axis=-1
    )


def rms_scaled(inputs, gains):
    return inputs * lax.rsqrt(jnp.mean(inputs * inputs, axis=-1, keepdims=True) + 1e-06) * gains


def shards(
    activations, norm_gain, master_weight, grad, moment, variance, query_gain, key_gain, prompt_len
):
    width_all = norm_gain.shape[0]
    grad_local = grad.astype(jnp.float32)
    sumsq = lax.psum(jnp.sum(grad_local * grad_local), ("group", "dp", "tensor"))
    clip_factor = 1.0 / jnp.sqrt(sumsq + 1e-12)
    clipped = grad_local * clip_factor
    moment_new = BETA_ONE * moment + (1.0 - BETA_ONE) * clipped
    variance_new = BETA_TWO * variance + (1.0 - BETA_TWO) * clipped * clipped
    step_size = STEP_SCALE * width_all ** (-0.5)
    updated = (master_weight - step_size * moment_new / (jnp.sqrt(variance_new) + 1e-08)).astype(
        jnp.bfloat16
    )
    gathered = lax.all_gather(activations, "tensor", axis=1, tiled=True)
    widened = gathered.astype(jnp.float32)
    row_scale = lax.rsqrt(jnp.mean(widened * widened, axis=-1, keepdims=True) + 1e-06)
    normed = (widened * row_scale * norm_gain).astype(jnp.bfloat16)
    seq_rows = normed.shape[0]
    slab_rows = updated.shape[0]
    head_dev = updated.shape[2] - 1
    head_size = updated.shape[3]
    query_cols = head_dev * head_size
    tensor_pos = lax.axis_index("tensor")
    is_even = tensor_pos % 2 == 0
    query_part = updated[:, 0, :head_dev].reshape(slab_rows, query_cols)
    own_part = updated[:, 0, head_dev]
    partner = from_partner(own_part, "tensor", 0)
    key_weight = jnp.where(is_even, own_part, partner)
    value_weight = jnp.where(is_even, partner, own_part)
    relayed = jnp.concatenate([query_part, key_weight, value_weight], axis=1)
    projected = jnp.dot(
        normed,
        lax.all_gather(relayed, ("group", "dp"), axis=0, tiled=True),
        preferred_element_type=jnp.float32,
    )
    cosine, sine = rope_tables(seq_rows, head_size)
    gain_row = lax.dynamic_slice_in_dim(key_gain, tensor_pos // 2, 1, 0)[0]
    query_proj = projected[:, :query_cols].reshape(seq_rows, head_dev, head_size)
    queries = rms_scaled(query_proj, query_gain)
    queries = (rotate(queries, cosine[:, None, :], sine[:, None, :]) * head_size ** (-0.5)).astype(
        jnp.bfloat16
    )
    key_rot = rotate(
        rms_scaled(projected[:, query_cols : query_cols + head_size], gain_row), cosine, sine
    ).astype(jnp.bfloat16)
    value_rows = projected[:, query_cols + head_size :].astype(jnp.bfloat16)
    scores = jnp.einsum("qhe,ke->hqk", queries, key_rot, preferred_element_type=jnp.float32)
    row_pos = jnp.arange(seq_rows, dtype=jnp.int32)[:, None]
    col_pos = jnp.arange(seq_rows, dtype=jnp.int32)[None, :]
    allowed = (col_pos <= row_pos) & (col_pos < prompt_len[0])
    scores = jnp.where(allowed[None], scores, -1e30)
    highest = jnp.max(scores, axis=-1, keepdims=True)
    weights = jnp.exp(scores - highest)
    weights = (weights / jnp.sum(weights, axis=-1, keepdims=True)).astype(jnp.bfloat16)
    output = jnp.einsum("hqk,ke->qhe", weights, value_rows, preferred_element_type=jnp.float32)
    return output.astype(jnp.bfloat16).reshape(seq_rows, query_cols)


def solution(mesh):
    in_specs = (
        P(("group", "dp"), "tensor"),
        P(),
        P(("group", "dp"), "tensor", None, None),
        P(("group", "dp"), "tensor", None, None),
        P(("group", "dp"), "tensor", None, None),
        P(("group", "dp"), "tensor", None, None),
        P("tensor", None),
        P(),
        P(("group", "dp")),
    )
    out_specs = P(("group", "dp"), "tensor")
    return jax.shard_map(shards, mesh=mesh, in_specs=in_specs, out_specs=out_specs, check_vma=False)
```

profile of v0, /device:TPU:2, one launch (start us, length us, event | category | flops | bytes accessed | tf_op | source)
XLA Modules:
  0.0 225.9 jit_solution(9197097616985687663)
XLA Ops:
  6.5 0.0 copy-start
  6.5 0.0 all-gather.3.cloned.1.call-start
  6.5 0.7 all-gather.3.cloned.1.call-update
  7.3 0.0 all-gather.5.cloned.1.call-start
  7.3 3.7 %multiply_reduce_fusion = f32[]{:T(128)} fusion(bf16[640,1,3,128]{3,0,2,1:T(8,128)(2,1)} %param.12), kind=kLoop, calls=%fused_computation.23 | loop fusion | flops 737279 | bytes 491524 | tf_op jit(solution)/shard_map/reduce_sum | solution.py:42
  11.0 46.3 %psum.7 = f32[]{:T(128)} all-reduce(f32[]{:T(128)} %multiply_reduce_fusion), channel_id=1, replica_groups=mesh['group'=4,'dp'=2,'tensor'=4] {'group','dp','tensor'}, use_global_device_ids=true, to_apply=%region_2.0 | all-reduce | flops 1 | bytes 8 | tf_op jit(solution)/shard_map/psum | solution.py:42
  57.9 7.4 %subtract_convert_fusion = bf16[640,1,3,128]{3,1,2,0:T(2,128)(2,1)S(1)} fusion(f32[640,1,3,128]{3,1,2,0:T(1,128)} %param.11, f32[640,1,3,128]{3,1,2,0:T(1,128)} %param.14, f32[640,1,3,128]{3,1,2,0:T(1,128)} %param.13, bf16[640,1,3,128]{3,0,2,1:T(8,128)(2,1)} %param.12, f32[]{:T(128)S(6)} %sqrt.6), kind=kLoop, calls=%fused_computation.22 | loop fusion | flops 3440640 | bytes 3932164 | tf_op jit(solution)/shard_map/convert_element_type | solution.py:48
  65.3 0.3 slice.38
  65.7 2.7 %collective-permute-start = (bf16[640,128]{1,0:T(8,128)(2,1)S(1)}, bf16[640,128]{1,0:T(8,128)(2,1)S(1)}, u32[]{:S(2)}, u32[]{:S(2)}) collective-permute-start(bf16[640,128]{1,0:T(8,128)(2,1)S(1)} %bitcast.49), channel_id=1, source_target_pairs={{0,1},{1,0},{2,3},{3,2},{4,5},{5,4},{6,7},{7,6},{8,9},{9,8},{10,11... | collective-permute-start | bytes 491528 | tf_op jit(solution)/shard_map/ppermute | solution.py:13
  68.4 2.2 slice_reduce_fusion
  70.6 13.4 %collective-permute-done = bf16[640,128]{1,0:T(8,128)(2,1)S(1)} collective-permute-done((bf16[640,128]{1,0:T(8,128)(2,1)S(1)}, bf16[640,128]{1,0:T(8,128)(2,1)S(1)}, u32[]{:S(2)}, u32[]{:S(2)}) %collective-permute-start) | collective-permute-done | bytes 163872 | tf_op jit(solution)/shard_map/ppermute | solution.py:13
  84.1 0.9 pad_maximum_fusion
  85.0 0.0 copy-start.2
  85.0 0.0 all-gather.5.cloned.1.call-update
  85.7 0.0 copy-done
  85.8 1.1 fusion.10
  86.8 66.7 %all-gather.3.cloned.1.call-done = bf16[768,5120]{1,0:T(8,128)(2,1)} async-done(((bf16[768,1280]{1,0:T(8,128)(2,1)}), bf16[768,5120]{1,0:T(8,128)(2,1)}) %all-gather.3.cloned.1.call-update) | async-done | bytes 7864336 | tf_op jit(solution)/shard_map/all_gather | solution.py:51
  153.5 4.8 %fusion.1 = f32[768]{0:T(1024)S(1)} fusion(bf16[768,5120]{1,0:T(8,128)(2,1)} %all-gather.3.cloned.1.call-done), kind=kLoop, calls=%fused_computation.3 | loop fusion | flops 11795712 | bytes 7867392 | tf_op jit(solution)/shard_map/reduce_sum | solution.py:53
  158.3 38.7 %all-gather.5.cloned.1.call-done = bf16[5120,512]{1,0:T(8,128)(2,1)} async-done(((bf16[640,512]{1,0:T(8,128)(2,1)}), bf16[5120,512]{1,0:T(8,128)(2,1)}) %all-gather.5.cloned.1.call-update) | async-done | bytes 5242896 | tf_op jit(solution)/shard_map/all_gather | solution.py:70
  197.0 0.0 copy-done.2
  197.0 9.8 %fusion.4 = f32[768,512]{0,1:T(8,128)S(1)} fusion(bf16[5120,512]{1,0:T(8,128)(2,1)} %all-gather.5.cloned.1.call-done, bf16[768,5120]{1,0:T(8,128)(2,1)} %all-gather.3.cloned.1.call-done, f32[5120]{0:T(1024)S(1)} %copy-done.2, f32[768]{0:T(1024)S(1)} %add_rsqrt_fusion.2), kind=kOutput, calls=%fused_computation.6 | convolution fusion | flops 4042260480 | bytes 14703616 | tf_op jit(solution)/shard_map/dot_general | solution.py:68
  206.8 0.0 copy-start.1
  206.8 0.1 slice.43
  206.9 0.1 multiply_reduce_fusion.1
  207.0 0.3 copy.11
  207.3 0.1 multiply_multiply_fusion.2
  207.4 0.8 subtract_convert_fusion.1
  208.2 0.2 copy.12
  208.4 0.2 copy.13
  208.6 0.0 copy-done.1
  208.6 0.3 multiply_multiply_fusion.1
  208.8 1.2 multiply_subtract_fusion
  210.0 5.3 %fusion.28 = (f32[2,768]{1,0:T(2,128)S(1)}, f32[2,768,768]{1,2,0:T(8,128)}) fusion(pred[768,768]{0,1:T(8,128)(4,1)} %fusion.10, bf16[768,64]{0,1:T(8,128)(2,1)S(1)} %get-tuple-element.8, bf16[768,64]{0,1:T(8,128)(2,1)S(1)} %get-tuple-element.7, f32[768,2,64]{2,0,1:T(8,128)} %get-tuple-element.6, f32[768,2,64]{2,0,1:T(8,128)S(1)} %get-tuple-element.5), kind=kOutput, calls=%fused_computation.57 | convolution fusion | flops 306512640 | bytes 6297600 | tf_op jit(solution)/shard_map/sub | solution.py:90
  215.3 2.8 %fusion.13 = bf16[128,2,768]{2,0,1:T(8,128)(2,1)S(1)} fusion(f32[2,768,768]{1,2,0:T(8,128)} %get-tuple-element.14, f32[2,768]{1,0:T(2,128)S(1)} %get-tuple-element.13, f32[768,512]{0,1:T(8,128)S(1)} %fusion.4), kind=kOutput, calls=%fused_computation.19 | convolution fusion | flops 304545792 | bytes 5314560 | tf_op jit(solution)/shard_map/hqk,ke->qhe/dot_general | solution.py:92
  218.2 0.9 copy.16
  (10 shorter events, 0.2 us)
Async XLA Ops:
  6.5 79.2 %copy-start = (f32[2,128]{1,0:T(2,128)S(1)}, f32[2,128]{1,0:T(2,128)}, u32[]{:S(2)}) copy-start(f32[2,128]{1,0:T(2,128)} %param.16) | copy-start | bytes 3076
  6.5 147.0 %all-gather.3.cloned.1.call-start = ((), (), s32[]{:S(2)}) async-start(), calls=%async_computation | async-start | bytes 9830400 | tf_op jit(solution)/shard_map/all_gather | solution.py:51
  7.3 189.8 %all-gather.5.cloned.1.call-start = ((), (), s32[]{:S(2)}) async-start(), calls=%async_computation.1 | async-start | bytes 5898240 | tf_op jit(solution)/shard_map/all_gather | solution.py:70
  65.7 18.4 %collective-permute-start = (bf16[640,128]{1,0:T(8,128)(2,1)S(1)}, bf16[640,128]{1,0:T(8,128)(2,1)S(1)}, u32[]{:S(2)}, u32[]{:S(2)}) collective-permute-start(bf16[640,128]{1,0:T(8,128)(2,1)S(1)} %bitcast.49), channel_id=1, source_target_pairs={{0,1},{1,0},{2,3},{3,2},{4,5},{5,4},{6,7},{7,6},{8,9},{9,8},{10,11... | collective-permute-start | bytes 491528 | tf_op jit(solution)/shard_map/ppermute | solution.py:13
  85.0 112.0 %copy-start.2 = (f32[5120]{0:T(1024)S(1)}, f32[5120]{0:T(1024)}, u32[]{:S(2)}) copy-start(f32[5120]{0:T(1024)} %param.10) | copy-start | bytes 61444
  206.8 1.8 copy-start.1
Sparse Core Ops, SparseCore 0:
  8.9 144.5 all-gather.2
  155.4 41.5 all-gather.4
where the time goes:
time: 228 us; the launch traced here: 226 us
  waiting for transfers between devices  119 us (52%)
  blocking collectives  46.3 us (20%)
  other arithmetic  20.4 us (9%)
  matrix products  17.9 us (8%)
  between operations  14.9 us (7%)
  local copies, waits for them, and re-layouts  4.21 us (2%)
  starting transfers between devices  2.75 us (1%)
    all_gather x1, waiting for transfers between devices, shards(): gathered = lax.all_gather(activations, 'tensor', axis=1, tiled=True)  66.7 us
    psum x1, blocking collectives, shards(): lax.psum(jnp.sum(grad_local * grad_local), ('group', 'dp', 'tensor'))  46.3 us
    all_gather x1, waiting for transfers between devices, shards(): lax.all_gather(relayed, ('group', 'dp'), axis=0, tiled=True)  38.7 us
    ppermute x1, waiting for transfers between devices, from_partner(): lax.ppermute(array, axis, [(i, i ^ 1 << distance) for i in range(lax.axis...  13.4 us
    dot_general x1, matrix products, shards(): jnp.dot(normed, lax.all_gather(relayed, ('group', 'dp'), axis=0, tiled=Tr...  9.76 us
    convert_element_type x1, other arithmetic, shards(): (master_weight - step_size * moment_new / (jnp.sqrt(variance_new) + 1e-08...  7.36 us
    sub x1, matrix products, shards(): weights = jnp.exp(scores - highest)  5.31 us
    reduce_sum x1, other arithmetic, shards(): jnp.mean(widened * widened, axis=-1, keepdims=True) + 1e-06  4.83 us
  transfers between devices with their start and end apart: 3, of which 3 were waited for; matrix products, arithmetic and copies ran while one was open for 9% of the time, Pallas kernels for 0%

commit v1 on v0

v1 whole, which is shorter than its diff:
```python
import functools

import jax
import jax.numpy as jnp
import numpy as np
from jax import lax
from jax.experimental import pallas as pl
from jax.experimental.pallas import tpu as pltpu
from jax.sharding import PartitionSpec as P

STEP_SCALE = 0.5
BETA_ONE = 0.9
BETA_TWO = 0.95
ROPE_BASE = 500000.0
MESH = pl.DeviceIdType.MESH
BF16 = jnp.bfloat16
F32 = jnp.float32


def rope_tables(length, head_size):
    positions = np.arange(length, dtype=np.float32)
    exponent = np.arange(head_size // 2, dtype=np.float32) * np.float32(2.0) / np.float32(head_size)
    inverse = np.power(np.float32(ROPE_BASE), -exponent).astype(np.float32)
    angles = (positions[:, None] * inverse[None, :]).astype(np.float32)
    cosine, sine = np.cos(angles), np.sin(angles)
    return (
        np.concatenate([cosine, cosine], axis=1).astype(np.float32),
        np.concatenate([-sine, sine], axis=1).astype(np.float32),
    )


def kernel(
    sizes,
    act_hbm, gain_ref, master_hbm, grad_hbm, moment_hbm, variance_hbm, query_gain_ref, key_gain_ref,
    cos_ref, sin_ref, len_ref,
    out_ref,
    act, normed, master, grad, moment, variance, q_own, kv_own, weights, parts, up, down, final, queries, keys, values,
    plane_sum, line_sum, row_sum,
    in_sem, plane_send, plane_recv, line_send, line_recv, row_send, row_recv,
    hub_send, w_recv, w_send, up_send, up_recv, down_send, down_recv,
):
    group_n, dp_n, tensor_n, width = sizes
    plane_n = group_n * dp_n
    chip_n = group_n // 2
    hubs = plane_n // tensor_n
    length, feat = act.shape
    slab_rows = grad.shape[1]
    blocks = weights.shape[0]
    head = 128
    chunk = 256 if length % 256 == 0 else length
    chunks = length // chunk

    g = lax.axis_index("group")
    d = lax.axis_index("dp")
    z = lax.axis_index("tensor")
    me = g * dp_n + d
    x, core = g // 2, g % 2

    def plane_peer(i):
        p = (me + i) % plane_n
        return p, (p // dp_n, p % dp_n, z)

    def line_peer(i):
        t = (z + i) % tensor_n
        return t, (g, d, t)

    loads = [
        pltpu.make_async_copy(src, dst, in_sem.at[i])
        for i, (src, dst) in enumerate(
            [(grad_hbm, grad), (act_hbm, act), (moment_hbm, moment), (variance_hbm, variance), (master_hbm, master)]
        )
    ]
    for load in loads:
        load.start()

    barrier = pltpu.get_barrier_semaphore()
    for i in range(1, plane_n):
        pl.semaphore_signal(barrier, inc=1, device_id=plane_peer(i)[1], device_id_type=MESH)
    for i in range(1, tensor_n):
        pl.semaphore_signal(barrier, inc=1, device_id=line_peer(i)[1], device_id_type=MESH)

    loads[0].wait()
    tile = jnp.zeros((8, head), F32)
    for s in range(3):
        piece = grad[s].astype(F32)
        tile += jnp.sum((piece * piece).reshape(slab_rows // 8, 8, head), axis=0)
    plane_sum[me] = tile
    pl.semaphore_wait(barrier, plane_n + tensor_n - 2)

    def exchange(buf, slot, dev, ssem, rsem):
        return pltpu.make_async_remote_copy(
            src_ref=buf.at[slot], dst_ref=buf.at[slot], send_sem=ssem, recv_sem=rsem.at[slot],
            device_id=dev, device_id_type=MESH,
        )

    for i in range(1, plane_n):
        exchange(plane_sum, me, plane_peer(i)[1], plane_send.at[i], plane_recv).start()

    loads[1].wait()
    for c in range(chunks):
        rows = pl.ds(c * chunk, chunk)
        wide = act[rows, :].astype(F32)
        column = jnp.sum(wide * wide, axis=1, keepdims=True)
        row_sum[z, :, rows] = jnp.broadcast_to(column, (chunk, head)).T[:8]
    for i in range(1, tensor_n):
        exchange(row_sum, z, line_peer(i)[1], row_send.at[i], row_recv).start()

    total = plane_sum[me]
    for i in range(1, plane_n):
        p, dev = plane_peer(i)
        exchange(plane_sum, p, dev, plane_send.at[i], plane_recv).wait_recv()
        total += plane_sum[p]
    line_sum[z] = total
    for i in range(1, tensor_n):
        exchange(line_sum, z, line_peer(i)[1], line_send.at[i], line_recv).start()
    for load in loads[2:]:
        load.wait()
    for i in range(1, tensor_n):
        t, dev = line_peer(i)
        exchange(line_sum, t, dev, line_send.at[i], line_recv).wait_recv()
        total += line_sum[t]
    sumsq = jnp.sum(jnp.sum(total, axis=0, keepdims=True), axis=1, keepdims=True)
    clip = 1.0 / jnp.sqrt(sumsq + 1e-12)

    step_size = STEP_SCALE * width ** (-0.5)

    def updated(s):
        clipped = grad[s].astype(F32) * clip
        rows = pl.ds(s, slab_rows, stride=3)
        moment_new = BETA_ONE * moment[rows, :] + (1.0 - BETA_ONE) * clipped
        variance_new = BETA_TWO * variance[rows, :] + (1.0 - BETA_TWO) * clipped * clipped
        return (master[rows, :] - step_size * moment_new / (jnp.sqrt(variance_new) + 1e-08)).astype(BF16)

    def q_block(t):
        return 3 * (t // 2) + 2 * (t % 2)

    def kv_block(t):
        return 3 * (t // 2) + 1

    def w_slot(r, t, part):
        rows = pl.ds(pl.multiple_of(r * slab_rows, 16), slab_rows)
        if part == 0:
            return weights.at[q_block(t), rows, :]
        return weights.at[kv_block(t), rows, pl.ds(pl.multiple_of((t % 2) * head, head), head)]

    owner, my_r = me // hubs, me % hubs

    def to_hub(part):
        return pltpu.make_async_remote_copy(
            src_ref=(q_own, kv_own)[part], dst_ref=w_slot(my_r, z, part), send_sem=hub_send.at[part],
            recv_sem=w_recv.at[my_r, z, part], device_id=(g, d, owner), device_id_type=MESH,
        )

    def place(part):
        @pl.when(z == owner)
        def _():
            w_slot(my_r, z, part)[...] = (q_own, kv_own)[part][...]

        @pl.when(z != owner)
        def _():
            to_hub(part).start()

    q_own[:, :head] = updated(0)
    q_own[:, head:] = updated(1)
    place(0)
    kv_own[...] = updated(2)
    place(1)

    square = row_sum[z]
    for i in range(1, tensor_n):
        t, dev = line_peer(i)
        exchange(row_sum, t, dev, row_send.at[i], row_recv).wait_recv()
        square += row_sum[t]
    scale_row = lax.rsqrt(square[:1] * (1.0 / width) + 1e-06)
    for c in range(chunks):
        rows = pl.ds(c * chunk, chunk)
        scale = jnp.broadcast_to(scale_row[:, c * chunk : (c + 1) * chunk], (head, chunk)).T[:, :1]
        normed[rows, :] = (act[rows, :].astype(F32) * scale * gain_ref[z]).astype(BF16)

    def forward(r, t, part, slot, dev):
        return pltpu.make_async_remote_copy(
            src_ref=w_slot(r, t, part), dst_ref=w_slot(r, t, part), send_sem=w_send.at[r, t, part, slot],
            recv_sem=w_recv.at[r, t, part], device_id=dev, device_id_type=MESH,
        )

    def forwards(r, t, part, act_on):
        hub = z * hubs + r
        hub_g, hub_d = hub // dp_n, hub % dp_n
        same_core = core == hub_g % 2
        at_hub = hub == me

        @pl.when(at_hub)
        def _():
            for i in range(1, chip_n):
                act_on(forward(r, t, part, i - 1, (((x + i) % chip_n) * 2 + core, d, z)))

        @pl.when(jnp.logical_and(same_core, d == hub_d))
        def _():
            for i in range(1, dp_n):
                act_on(forward(r, t, part, chip_n - 2 + i, (g, (d + i) % dp_n, z)))

        @pl.when(same_core)
        def _():
            act_on(forward(r, t, part, chip_n + dp_n - 2, (x * 2 + 1 - core, d, z)))

    def start(copy):
        copy.start()

    def wait_send(copy):
        copy.wait_send()

    def chain(buf, b, c, dev_z, ssem, rsem):
        rows = pl.ds(pl.multiple_of(c * chunk, 16), chunk)
        return pltpu.make_async_remote_copy(
            src_ref=buf.at[b, rows, :], dst_ref=buf.at[b, rows, :], send_sem=ssem.at[b, c], recv_sem=rsem.at[b, c],
            device_id=(g, d, dev_z), device_id_type=MESH,
        )

    def chain_up(b, c):
        return chain(up, b, c, jnp.minimum(z + 1, tensor_n - 1), up_send, up_recv)

    def chain_down(b, c):
        return chain(down, b, c, jnp.maximum(z - 1, 0), down_send, down_recv)

    def span(b):
        pair, j = b // 3, b % 3
        return 2 * pair + j // 2, 2 * pair + (j + 1) // 2

    def multiply(b):
        low, high = span(b)

        @pl.loop(0, chunks)
        def _(c):
            rows = pl.ds(pl.multiple_of(c * chunk, 16), chunk)
            parts[b, rows, :] = jnp.dot(normed[rows, :], weights[b], preferred_element_type=F32)

            @pl.when(jnp.logical_and(z == 0, z < high))
            def _():
                up[b, rows, :] = parts[b, rows, :].astype(BF16)
                chain_up(b, c).start()

            @pl.when(jnp.logical_and(z == tensor_n - 1, z > low))
            def _():
                down[b, rows, :] = parts[b, rows, :].astype(BF16)
                chain_down(b, c).start()

    @pl.loop(0, 2 * tensor_n - 1)
    def _(k):
        distance = (k + 1) // 2
        t = z + distance * (2 * (k % 2) - 1)

        @pl.when(jnp.logical_and(t >= 0, t < tensor_n))
        def _():
            for r in range(hubs):
                for part in range(2):
                    @pl.when(jnp.logical_not(jnp.logical_and(z * hubs + r == me, t == z)))
                    def _():
                        forward(r, t, part, 0, (g, d, z)).wait_recv()

                    forwards(r, t, part, start)
            multiply(q_block(t))
            mate = t + 1 - 2 * (t % 2)
            offset = mate - z
            rank = jnp.where(offset > 0, 2 * offset - 1, -2 * offset)

            @pl.when(rank < k)
            def _():
                multiply(kv_block(t))

    mine = (q_block(z), kv_block(z))
    for slot in range(2):
        final[slot] = parts[mine[slot]]

    @pl.loop(0, blocks)
    def _(i):
        def hop(b, c, buf, copy, receives, sends):
            low, high = span(b)
            rows = pl.ds(pl.multiple_of(c * chunk, 16), chunk)

            @pl.when(receives)
            def _():
                copy(b, c).wait_recv()

                @pl.when(jnp.logical_and(low <= z, z <= high))
                def _():
                    slot = 1 - (b % 3 != 1).astype(jnp.int32)
                    final[slot, rows, :] += buf[b, rows, :].astype(F32)

                @pl.when(sends)
                def _():
                    buf[b, rows, :] = (parts[b, rows, :] + buf[b, rows, :].astype(F32)).astype(BF16)
                    copy(b, c).start()

        @pl.loop(0, chunks)
        def _(c):
            low, high = span(i)
            hop(i, c, up, chain_up, jnp.logical_and(z > 0, z <= high), z < high)
            j = blocks - 1 - i
            low, high = span(j)
            hop(j, c, down, chain_down, jnp.logical_and(z < tensor_n - 1, z >= low), z > low)

    def prepared(raw, gains, rows):
        scaled = raw * lax.rsqrt(jnp.mean(raw * raw, axis=1, keepdims=True) + 1e-06) * gains
        return scaled * cos_ref[rows, :] + pltpu.roll(scaled, head // 2, 1) * sin_ref[rows, :]

    key_gain = key_gain_ref[pl.ds(z // 2, 1), :]
    for c in range(chunks):
        rows = pl.ds(c * chunk, chunk)
        for j in range(2):
            raw = final[0, rows, j * head : (j + 1) * head]
            queries[j, rows, :] = (prepared(raw, query_gain_ref[j : j + 1, :], rows) * head ** (-0.5)).astype(BF16)
        keys[rows, :] = prepared(final[1, rows, :head], key_gain, rows).astype(BF16)
        values[rows, :] = final[1, rows, head:].astype(BF16)
    live = len_ref[0]
    for c in range(chunks):
        rows = pl.ds(c * chunk, chunk)
        seen = (c + 1) * chunk
        row_pos = lax.broadcasted_iota(jnp.int32, (chunk, seen), 0) + c * chunk
        col_pos = lax.broadcasted_iota(jnp.int32, (chunk, seen), 1)
        allowed = jnp.logical_and(col_pos <= row_pos, col_pos < live)
        for j in range(2):
            scores = lax.dot_general(
                queries[j, rows, :], keys[:seen, :], (((1,), (1,)), ((), ())), preferred_element_type=F32
            )
            scores = jnp.where(allowed, scores, -1e30)
            exps = jnp.exp(scores - jnp.max(scores, axis=1, keepdims=True))
            probs = (exps / jnp.sum(exps, axis=1, keepdims=True)).astype(BF16)
            out_ref[rows, j * head : (j + 1) * head] = jnp.dot(
                probs, values[:seen, :], preferred_element_type=F32
            ).astype(BF16)

    for i in range(1, plane_n):
        exchange(plane_sum, me, plane_peer(i)[1], plane_send.at[i], plane_recv).wait_send()
    for i in range(1, tensor_n):
        dev = line_peer(i)[1]
        exchange(line_sum, z, dev, line_send.at[i], line_recv).wait_send()
        exchange(row_sum, z, dev, row_send.at[i], row_recv).wait_send()

    @pl.when(z != owner)
    def _():
        to_hub(0).wait_send()
        to_hub(1).wait_send()

    @pl.loop(0, tensor_n)
    def _(t):
        for r in range(hubs):
            for part in range(2):
                forwards(r, t, part, wait_send)

    @pl.loop(0, blocks)
    def _(b):
        low, high = span(b)

        @pl.loop(0, chunks)
        def _(c):
            @pl.when(z < high)
            def _():
                chain_up(b, c).wait_send()

            @pl.when(z > low)
            def _():
                chain_down(b, c).wait_send()


def shards(sizes, activations, norm_gain, master_weight, grad, moment, variance, query_gain, key_gain, prompt_len):
    group_n, dp_n, tensor_n = sizes
    plane_n = group_n * dp_n
    hubs = plane_n // tensor_n
    width = norm_gain.shape[0]
    length, feat = activations.shape
    slab_rows, _, slots, head = master_weight.shape
    pair = 2 * head
    blocks = 3 * tensor_n // 2
    chunk = 256 if length % 256 == 0 else length
    chunks = length // chunk
    cosine, sine = rope_tables(length, head)

    def flat(array):
        return array.reshape(slab_rows * slots, head)

    hbm = pl.BlockSpec(memory_space=pl.ANY)
    vmem = pl.BlockSpec(memory_space=pltpu.VMEM)
    dma = pltpu.SemaphoreType.DMA
    return pl.pallas_call(
        functools.partial(kernel, (group_n, dp_n, tensor_n, width)),
        out_shape=jax.ShapeDtypeStruct((length, pair), BF16),
        in_specs=[hbm, vmem, hbm, hbm, hbm, hbm, vmem, vmem, vmem, vmem, pl.BlockSpec(memory_space=pltpu.SMEM)],
        out_specs=vmem,
        scratch_shapes=[
            pltpu.VMEM((length, feat), BF16),
            pltpu.VMEM((length, feat), BF16),
            pltpu.VMEM((slab_rows * slots, head), F32),
            pltpu.VMEM((slots, slab_rows, head), BF16),
            pltpu.VMEM((slab_rows * slots, head), F32),
            pltpu.VMEM((slab_rows * slots, head), F32),
            pltpu.VMEM((slab_rows, pair), BF16),
            pltpu.VMEM((slab_rows, head), BF16),
            pltpu.VMEM((blocks, feat, pair), BF16),
            pltpu.VMEM((blocks, length, pair), F32),
            pltpu.VMEM((blocks, length, pair), BF16),
            pltpu.VMEM((blocks, length, pair), BF16),
            pltpu.VMEM((2, length, pair), F32),
            pltpu.VMEM((2, length, head), BF16),
            pltpu.VMEM((length, head), BF16),
            pltpu.VMEM((length, head), BF16),
            pltpu.VMEM((plane_n, 8, head), F32),
            pltpu.VMEM((tensor_n, 8, head), F32),
            pltpu.VMEM((tensor_n, 8, length), F32),
            dma((5,)),
            dma((plane_n,)),
            dma((plane_n,)),
            dma((tensor_n,)),
            dma((tensor_n,)),
            dma((tensor_n,)),
            dma((tensor_n,)),
            dma((2,)),
            dma((hubs, tensor_n, 2)),
            dma((hubs, tensor_n, 2, group_n // 2 + dp_n - 1)),
            dma((blocks, chunks)),
            dma((blocks, chunks)),
            dma((blocks, chunks)),
            dma((blocks, chunks)),
        ],
        compiler_params=pltpu.CompilerParams(
            collective_id=0, has_side_effects=True, vmem_limit_bytes=60 * 1024 * 1024
        ),
        name="step_and_prefill",
    )(
        activations,
        norm_gain.reshape(tensor_n, 1, feat),
        flat(master_weight),
        jnp.transpose(grad.reshape(slab_rows, slots, head), (1, 0, 2)),
        flat(moment),
        flat(variance),
        query_gain,
        key_gain,
        cosine,
        sine,
        prompt_len,
    )


def solution(mesh):
    in_specs = (
        P(("group", "dp"), "tensor"),
        P(),
        P(("group", "dp"), "tensor", None, None),
        P(("group", "dp"), "tensor", None, None),
        P(("group", "dp"), "tensor", None, None),
        P(("group", "dp"), "tensor", None, None),
        P("tensor", None),
        P(),
        P(("group", "dp")),
    )
    out_specs = P(("group", "dp"), "tensor")
    sizes = tuple(mesh.shape[axis] for axis in ("group", "dp", "tensor"))
    return jax.shard_map(
        functools.partial(shards, sizes), mesh=mesh, in_specs=in_specs, out_specs=out_specs, check_vma=False
    )
```

time: 228 us -> 179 us (0.79)
  the two profiles are of different devices: /device:TPU:2 before, /device:TPU:0 now
where the time goes in v1:
time: 179 us
  Pallas kernels  176 us (98%)
    pallas_call x1, Pallas kernels, shards(): pl.pallas_call(functools.partial(kernel, (group_n, dp_n, tensor_n, width)...  176 us

profile of v1, /device:TPU:0, one launch (start us, length us, event | category | flops | bytes accessed | tf_op | source)
XLA Modules:
  0.0 178.8 jit_solution(11902458268191396308)
XLA Ops:
  0.7 176.4 %step_and_prefill.1 = bf16[768,256]{1,0:T(8,128)(2,1)} custom-call(bf16[768,1280]{1,0:T(8,128)(2,1)} %act_hbm.1, f32[4,1,1280]{2,1,0:T(1,128)} %bitcast.11, f32[1920,128]{1,0:T(8,128)} %bitcast.7, bf16[3,640,128]{2,1,0:T(8,128)(2,1)} %bitcast.10, f32[1920,128]{1,0:T(8,128)} %bitcast.8, f32[1920,128]{1,0:T(8,128)} %bitcast.9, f32[2,128]{1,0:T(2,128)} %query_gain_ref.1, ...), custom_call_target="tpu_custom_call" | custom-call | tf_op jit(solution)/shard_map/step_and_prefill/pallas_call | solution.py:384
  177.1 1.8 copy.14

commit v2 on v1

--- a/solution.py
+++ b/solution.py
@@ -34,7 +34,7 @@
     act_hbm, gain_ref, master_hbm, grad_hbm, moment_hbm, variance_hbm, query_gain_ref, key_gain_ref,
     cos_ref, sin_ref, len_ref,
     out_ref,
-    act, normed, master, grad, moment, variance, q_own, kv_own, weights, parts, up, down, final, queries, keys, values,
+    act, normed, master, grad, moment, variance, own, weights, parts, up, down, final, keys, values,
     plane_sum, line_sum, row_sum,
     in_sem, plane_send, plane_recv, line_send, line_recv, row_send, row_recv,
     hub_send, w_recv, w_send, up_send, up_recv, down_send, down_recv,
@@ -49,6 +49,8 @@
     head = 128
     chunk = 256 if length % 256 == 0 else length
     chunks = length // chunk
+    piece_rows = chunk // 2
+    pieces = length // piece_rows
 
     g = lax.axis_index("group")
     d = lax.axis_index("dp")
@@ -139,32 +141,30 @@
 
     def w_slot(r, t, part):
         rows = pl.ds(pl.multiple_of(r * slab_rows, 16), slab_rows)
-        if part == 0:
-            return weights.at[q_block(t), rows, :]
+        if part < 2:
+            return weights.at[q_block(t), rows, part * head : (part + 1) * head]
         return weights.at[kv_block(t), rows, pl.ds(pl.multiple_of((t % 2) * head, head), head)]
 
     owner, my_r = me // hubs, me % hubs
 
     def to_hub(part):
         return pltpu.make_async_remote_copy(
-            src_ref=(q_own, kv_own)[part], dst_ref=w_slot(my_r, z, part), send_sem=hub_send.at[part],
+            src_ref=own.at[part], dst_ref=w_slot(my_r, z, part), send_sem=hub_send.at[part],
             recv_sem=w_recv.at[my_r, z, part], device_id=(g, d, owner), device_id_type=MESH,
         )
 
     def place(part):
         @pl.when(z == owner)
         def _():
-            w_slot(my_r, z, part)[...] = (q_own, kv_own)[part][...]
+            w_slot(my_r, z, part)[...] = own[part]
 
         @pl.when(z != owner)
         def _():
             to_hub(part).start()
 
-    q_own[:, :head] = updated(0)
-    q_own[:, head:] = updated(1)
-    place(0)
-    kv_own[...] = updated(2)
-    place(1)
+    for part in range(3):
+        own[part] = updated(part)
+        place(part)
 
     square = row_sum[z]
     for i in range(1, tensor_n):
@@ -210,7 +210,7 @@
         copy.wait_send()
 
     def chain(buf, b, c, dev_z, ssem, rsem):
-        rows = pl.ds(pl.multiple_of(c * chunk, 16), chunk)
+        rows = pl.ds(pl.multiple_of(c * piece_rows, 16), piece_rows)
         return pltpu.make_async_remote_copy(
             src_ref=buf.at[b, rows, :], dst_ref=buf.at[b, rows, :], send_sem=ssem.at[b, c], recv_sem=rsem.at[b, c],
             device_id=(g, d, dev_z), device_id_type=MESH,
@@ -226,23 +226,25 @@
         pair, j = b // 3, b % 3
         return 2 * pair + j // 2, 2 * pair + (j + 1) // 2
 
-    def multiply(b):
-        low, high = span(b)
-
+    def multiply(*todo):
         @pl.loop(0, chunks)
         def _(c):
             rows = pl.ds(pl.multiple_of(c * chunk, 16), chunk)
-            parts[b, rows, :] = jnp.dot(normed[rows, :], weights[b], preferred_element_type=F32)
-
-            @pl.when(jnp.logical_and(z == 0, z < high))
-            def _():
-                up[b, rows, :] = parts[b, rows, :].astype(BF16)
-                chain_up(b, c).start()
-
-            @pl.when(jnp.logical_and(z == tensor_n - 1, z > low))
-            def _():
-                down[b, rows, :] = parts[b, rows, :].astype(BF16)
-                chain_down(b, c).start()
+            for b in todo:
+                low, high = span(b)
+                parts[b, rows, :] = jnp.dot(normed[rows, :], weights[b], preferred_element_type=F32)
+
+                @pl.when(jnp.logical_and(z == 0, z < high))
+                def _():
+                    up[b, rows, :] = parts[b, rows, :].astype(BF16)
+                    for half in range(2):
+                        chain_up(b, 2 * c + half).start()
+
+                @pl.when(jnp.logical_and(z == tensor_n - 1, z > low))
+                def _():
+                    down[b, rows, :] = parts[b, rows, :].astype(BF16)
+                    for half in range(2):
+                        chain_down(b, 2 * c + half).start()
 
     @pl.loop(0, 2 * tensor_n - 1)
     def _(k):
@@ -251,77 +253,88 @@
 
         @pl.when(jnp.logical_and(t >= 0, t < tensor_n))
         def _():
-            for r in range(hubs):
-                for part in range(2):
+            for i in range(hubs):
+                r = (d + i) % hubs
+                for part in range(3):
                     @pl.when(jnp.logical_not(jnp.logical_and(z * hubs + r == me, t == z)))
                     def _():
                         forward(r, t, part, 0, (g, d, z)).wait_recv()
 
                     forwards(r, t, part, start)
-            multiply(q_block(t))
             mate = t + 1 - 2 * (t % 2)
             offset = mate - z
             rank = jnp.where(offset > 0, 2 * offset - 1, -2 * offset)
 
             @pl.when(rank < k)
             def _():
-                multiply(kv_block(t))
+                multiply(kv_block(t), q_block(t))
+
+            @pl.when(rank >= k)
+            def _():
+                multiply(q_block(t))
 
     mine = (q_block(z), kv_block(z))
     for slot in range(2):
         final[slot] = parts[mine[slot]]
 
-    @pl.loop(0, blocks)
+    def hop(b, c, buf, copy, receives, sends):
+        low, high = span(b)
+        rows = pl.ds(pl.multiple_of(c * piece_rows, 16), piece_rows)
+
+        @pl.when(receives)
+        def _():
+            copy(b, c).wait_recv()
+            arrived = buf[b, rows, :].astype(F32)
+
+            @pl.when(sends)
+            def _():
+                buf[b, rows, :] = (parts[b, rows, :] + arrived).astype(BF16)
+                copy(b, c).start()
+
+            @pl.when(jnp.logical_and(low <= z, z <= high))
+            def _():
+                slot = 1 - abs(b % 3 - 1)
+                final[slot, rows, :] += arrived
+
+    def hop_up(b, c):
+        high = span(b)[1]
+        hop(b, c, up, chain_up, jnp.logical_and(z > 0, z <= high), z < high)
+
+    def hop_down(b, c):
+        low = span(b)[0]
+        hop(b, c, down, chain_down, jnp.logical_and(z < tensor_n - 1, z >= low), z > low)
+
+    @pl.loop(0, blocks - 2)
     def _(i):
-        def hop(b, c, buf, copy, receives, sends):
-            low, high = span(b)
-            rows = pl.ds(pl.multiple_of(c * chunk, 16), chunk)
-
-            @pl.when(receives)
-            def _():
-                copy(b, c).wait_recv()
-
-                @pl.when(jnp.logical_and(low <= z, z <= high))
-                def _():
-                    slot = 1 - (b % 3 != 1).astype(jnp.int32)
-                    final[slot, rows, :] += buf[b, rows, :].astype(F32)
-
-                @pl.when(sends)
-                def _():
-                    buf[b, rows, :] = (parts[b, rows, :] + buf[b, rows, :].astype(F32)).astype(BF16)
-                    copy(b, c).start()
-
-        @pl.loop(0, chunks)
+        @pl.loop(0, pieces)
         def _(c):
-            low, high = span(i)
-            hop(i, c, up, chain_up, jnp.logical_and(z > 0, z <= high), z < high)
-            j = blocks - 1 - i
-            low, high = span(j)
-            hop(j, c, down, chain_down, jnp.logical_and(z < tensor_n - 1, z >= low), z > low)
+            hop_up(i, c)
+            hop_down(blocks - 1 - i, c)
 
     def prepared(raw, gains, rows):
         scaled = raw * lax.rsqrt(jnp.mean(raw * raw, axis=1, keepdims=True) + 1e-06) * gains
         return scaled * cos_ref[rows, :] + pltpu.roll(scaled, head // 2, 1) * sin_ref[rows, :]
 
     key_gain = key_gain_ref[pl.ds(z // 2, 1), :]
+    live = len_ref[0]
     for c in range(chunks):
+        @pl.loop(2 * c, 2 * c + 2)
+        def _(p):
+            for i in range(2):
+                hop_up(blocks - 2 + i, p)
+                hop_down(1 - i, p)
+
         rows = pl.ds(c * chunk, chunk)
-        for j in range(2):
-            raw = final[0, rows, j * head : (j + 1) * head]
-            queries[j, rows, :] = (prepared(raw, query_gain_ref[j : j + 1, :], rows) * head ** (-0.5)).astype(BF16)
+        seen = (c + 1) * chunk
         keys[rows, :] = prepared(final[1, rows, :head], key_gain, rows).astype(BF16)
         values[rows, :] = final[1, rows, head:].astype(BF16)
-    live = len_ref[0]
-    for c in range(chunks):
-        rows = pl.ds(c * chunk, chunk)
-        seen = (c + 1) * chunk
         row_pos = lax.broadcasted_iota(jnp.int32, (chunk, seen), 0) + c * chunk
         col_pos = lax.broadcasted_iota(jnp.int32, (chunk, seen), 1)
         allowed = jnp.logical_and(col_pos <= row_pos, col_pos < live)
         for j in range(2):
-            scores = lax.dot_general(
-                queries[j, rows, :], keys[:seen, :], (((1,), (1,)), ((), ())), preferred_element_type=F32
-            )
+            raw = final[0, rows, j * head : (j + 1) * head]
+            query = (prepared(raw, query_gain_ref[j : j + 1, :], rows) * head ** (-0.5)).astype(BF16)
+            scores = lax.dot_general(query, keys[:seen, :], (((1,), (1,)), ((), ())), preferred_element_type=F32)
             scores = jnp.where(allowed, scores, -1e30)
             exps = jnp.exp(scores - jnp.max(scores, axis=1, keepdims=True))
             probs = (exps / jnp.sum(exps, axis=1, keepdims=True)).astype(BF16)
@@ -338,20 +351,20 @@
 
     @pl.when(z != owner)
     def _():
-        to_hub(0).wait_send()
-        to_hub(1).wait_send()
+        for part in range(3):
+            to_hub(part).wait_send()
 
     @pl.loop(0, tensor_n)
     def _(t):
         for r in range(hubs):
-            for part in range(2):
+            for part in range(3):
                 forwards(r, t, part, wait_send)
 
     @pl.loop(0, blocks)
     def _(b):
         low, high = span(b)
 
-        @pl.loop(0, chunks)
+        @pl.loop(0, pieces)
         def _(c):
             @pl.when(z < high)
             def _():
@@ -372,7 +385,7 @@
     pair = 2 * head
     blocks = 3 * tensor_n // 2
     chunk = 256 if length % 256 == 0 else length
-    chunks = length // chunk
+    pieces = 2 * (length // chunk)
     cosine, sine = rope_tables(length, head)
 
     def flat(array):
@@ -393,14 +406,12 @@
             pltpu.VMEM((slots, slab_rows, head), BF16),
             pltpu.VMEM((slab_rows * slots, head), F32),
             pltpu.VMEM((slab_rows * slots, head), F32),
-            pltpu.VMEM((slab_rows, pair), BF16),
-            pltpu.VMEM((slab_rows, head), BF16),
+            pltpu.VMEM((slots, slab_rows, head), BF16),
             pltpu.VMEM((blocks, feat, pair), BF16),
             pltpu.VMEM((blocks, length, pair), F32),
             pltpu.VMEM((blocks, length, pair), BF16),
             pltpu.VMEM((blocks, length, pair), BF16),
             pltpu.VMEM((2, length, pair), F32),
-            pltpu.VMEM((2, length, head), BF16),
             pltpu.VMEM((length, head), BF16),
             pltpu.VMEM((length, head), BF16),
             pltpu.VMEM((plane_n, 8, head), F32),
@@ -413,13 +424,13 @@
             dma((tensor_n,)),
             dma((tensor_n,)),
             dma((tensor_n,)),
-            dma((2,)),
-            dma((hubs, tensor_n, 2)),
-            dma((hubs, tensor_n, 2, group_n // 2 + dp_n - 1)),
-            dma((blocks, chunks)),
-            dma((blocks, chunks)),
-            dma((blocks, chunks)),
-            dma((blocks, chunks)),
+            dma((3,)),
+            dma((hubs, tensor_n, 3)),
+            dma((hubs, tensor_n, 3, group_n // 2 + dp_n - 1)),
+            dma((blocks, pieces)),
+            dma((blocks, pieces)),
+            dma((blocks, pieces)),
+            dma((blocks, pieces)),
         ],
         compiler_params=pltpu.CompilerParams(
             collective_id=0, has_side_effects=True, vmem_limit_bytes=60 * 1024 * 1024

time: 179 us -> 200 us (1.12)
  the two profiles are of different devices: /device:TPU:0 before, /device:TPU:2 now
where the time goes in v2:
time: 200 us
  Pallas kernels  197 us (98%)
    pallas_call x1, Pallas kernels, shards(): pl.pallas_call(functools.partial(kernel, (group_n, dp_n, tensor_n, width)...  197 us

profile of v2, /device:TPU:2, one launch (start us, length us, event | category | flops | bytes accessed | tf_op | source)
XLA Modules:
  0.0 199.7 jit_solution(7415723150338771855)
XLA Ops:
  0.7 197.2 %step_and_prefill.1 = bf16[768,256]{1,0:T(8,128)(2,1)} custom-call(bf16[768,1280]{1,0:T(8,128)(2,1)} %act_hbm.1, f32[4,1,1280]{2,1,0:T(1,128)} %bitcast.11, f32[1920,128]{1,0:T(8,128)} %bitcast.7, bf16[3,640,128]{2,1,0:T(8,128)(2,1)} %bitcast.10, f32[1920,128]{1,0:T(8,128)} %bitcast.8, f32[1920,128]{1,0:T(8,128)} %bitcast.9, f32[2,128]{1,0:T(2,128)} %query_gain_ref.1, ...), custom_call_target="tpu_custom_call" | custom-call | tf_op jit(solution)/shard_map/step_and_prefill/pallas_call | solution.py:397
  197.9 1.8 copy.14

commit v3 on v2

--- a/solution.py
+++ b/solution.py
@@ -45,7 +45,7 @@
     hubs = plane_n // tensor_n
     length, feat = act.shape
     slab_rows = grad.shape[1]
-    blocks = weights.shape[0]
+    blocks = weights.shape[0] // 2
     head = 128
     chunk = 256 if length % 256 == 0 else length
     chunks = length // chunk
@@ -141,9 +141,8 @@
 
     def w_slot(r, t, part):
         rows = pl.ds(pl.multiple_of(r * slab_rows, 16), slab_rows)
-        if part < 2:
-            return weights.at[q_block(t), rows, part * head : (part + 1) * head]
-        return weights.at[kv_block(t), rows, pl.ds(pl.multiple_of((t % 2) * head, head), head)]
+        column = 2 * q_block(t) + part if part < 2 else 2 * kv_block(t) + t % 2
+        return weights.at[column, rows, :]
 
     owner, my_r = me // hubs, me % hubs
 
@@ -232,7 +231,8 @@
             rows = pl.ds(pl.multiple_of(c * chunk, 16), chunk)
             for b in todo:
                 low, high = span(b)
-                parts[b, rows, :] = jnp.dot(normed[rows, :], weights[b], preferred_element_type=F32)
+                both = jnp.concatenate([weights[2 * b], weights[2 * b + 1]], axis=1)
+                parts[b, rows, :] = jnp.dot(normed[rows, :], both, preferred_element_type=F32)
 
                 @pl.when(jnp.logical_and(z == 0, z < high))
                 def _():
@@ -407,7 +407,7 @@
             pltpu.VMEM((slab_rows * slots, head), F32),
             pltpu.VMEM((slab_rows * slots, head), F32),
             pltpu.VMEM((slots, slab_rows, head), BF16),
-            pltpu.VMEM((blocks, feat, pair), BF16),
+            pltpu.VMEM((2 * blocks, feat, head), BF16),
             pltpu.VMEM((blocks, length, pair), F32),
             pltpu.VMEM((blocks, length, pair), BF16),
             pltpu.VMEM((blocks, length, pair), BF16),

time: 200 us -> 200 us (level)
  no operation moved by 1% of the time
where the time goes in v3:
time: 200 us
  Pallas kernels  197 us (98%)
    pallas_call x1, Pallas kernels, shards(): pl.pallas_call(functools.partial(kernel, (group_n, dp_n, tensor_n, width)...  197 us

profile of v3, /device:TPU:2, one launch (start us, length us, event | category | flops | bytes accessed | tf_op | source)
XLA Modules:
  0.0 199.9 jit_solution(16332426193349479704)
XLA Ops:
  0.7 197.5 %step_and_prefill.1 = bf16[768,256]{1,0:T(8,128)(2,1)} custom-call(bf16[768,1280]{1,0:T(8,128)(2,1)} %act_hbm.1, f32[4,1,1280]{2,1,0:T(1,128)} %bitcast.11, f32[1920,128]{1,0:T(8,128)} %bitcast.7, bf16[3,640,128]{2,1,0:T(8,128)(2,1)} %bitcast.10, f32[1920,128]{1,0:T(8,128)} %bitcast.8, f32[1920,128]{1,0:T(8,128)} %bitcast.9, f32[2,128]{1,0:T(2,128)} %query_gain_ref.1, ...), custom_call_target="tpu_custom_call" | custom-call | tf_op jit(solution)/shard_map/step_and_prefill/pallas_call | solution.py:397
  198.1 1.8 copy.14

commit v4 on v3

--- a/solution.py
+++ b/solution.py
@@ -246,32 +246,44 @@
                     for half in range(2):
                         chain_down(b, 2 * c + half).start()
 
-    @pl.loop(0, 2 * tensor_n - 1)
-    def _(k):
-        distance = (k + 1) // 2
-        t = z + distance * (2 * (k % 2) - 1)
-
-        @pl.when(jnp.logical_and(t >= 0, t < tensor_n))
-        def _():
-            for i in range(hubs):
-                r = (d + i) % hubs
-                for part in range(3):
-                    @pl.when(jnp.logical_not(jnp.logical_and(z * hubs + r == me, t == z)))
-                    def _():
-                        forward(r, t, part, 0, (g, d, z)).wait_recv()
-
-                    forwards(r, t, part, start)
-            mate = t + 1 - 2 * (t % 2)
-            offset = mate - z
-            rank = jnp.where(offset > 0, 2 * offset - 1, -2 * offset)
-
-            @pl.when(rank < k)
+    def slab(j):
+        room = jnp.minimum(z, tensor_n - 1 - z)
+        near = z + ((j + 1) // 2) * (2 * (j % 2) - 1)
+        far = jnp.where(z < tensor_n - 1 - z, j, tensor_n - 1 - j)
+        return jnp.where(j <= 2 * room, near, far)
+
+    def rank(t):
+        return jnp.where(t > z, 2 * (t - z) - 1, 2 * (z - t))
+
+    def pass_on(t, i):
+        r = (d + i) % hubs
+        for part in range(3):
+            @pl.when(jnp.logical_not(jnp.logical_and(z * hubs + r == me, t == z)))
             def _():
-                multiply(kv_block(t), q_block(t))
-
-            @pl.when(rank >= k)
-            def _():
-                multiply(q_block(t))
+                forward(r, t, part, 0, (g, d, z)).wait_recv()
+
+            forwards(r, t, part, start)
+
+    pass_on(slab(0), 0)
+
+    @pl.loop(0, tensor_n)
+    def _(j):
+        @pl.when(j + 1 < tensor_n)
+        def _():
+            pass_on(slab(jnp.minimum(j + 1, tensor_n - 1)), 0)
+
+        t = slab(j)
+        for i in range(1, hubs):
+            pass_on(t, i)
+        complete = rank(t + 1 - 2 * (t % 2)) < rank(t)
+
+        @pl.when(complete)
+        def _():
+            multiply(kv_block(t), q_block(t))
+
+        @pl.when(jnp.logical_not(complete))
+        def _():
+            multiply(q_block(t))
 
     mine = (q_block(z), kv_block(z))
     for slot in range(2):
@@ -304,12 +316,26 @@
         low = span(b)[0]
         hop(b, c, down, chain_down, jnp.logical_and(z < tensor_n - 1, z >= low), z > low)
 
-    @pl.loop(0, blocks - 2)
-    def _(i):
-        @pl.loop(0, pieces)
-        def _(c):
-            hop_up(i, c)
-            hop_down(blocks - 1 - i, c)
+    early = (blocks - 2) * pieces
+    items = blocks * pieces
+    lag = 3 * jnp.abs(tensor_n - 1 - 2 * z)
+    up_lag = jnp.where(2 * z < tensor_n, 0, lag)
+    down_lag = lag - up_lag
+
+    def item(n):
+        late = n - early
+        b = jnp.where(late < 0, n // pieces, blocks - 2 + late % 2)
+        return b, jnp.where(late < 0, n % pieces, late // 2)
+
+    def step(n):
+        def one(n, hop_one, mirror):
+            @pl.when(jnp.logical_and(n >= 0, n < items))
+            def _():
+                b, c = item(jnp.clip(n, 0, items - 1))
+                hop_one(blocks - 1 - b if mirror else b, c)
+
+        one(n - up_lag, hop_up, False)
+        one(n - down_lag, hop_down, True)
 
     def prepared(raw, gains, rows):
         scaled = raw * lax.rsqrt(jnp.mean(raw * raw, axis=1, keepdims=True) + 1e-06) * gains
@@ -317,13 +343,8 @@
 
     key_gain = key_gain_ref[pl.ds(z // 2, 1), :]
     live = len_ref[0]
-    for c in range(chunks):
-        @pl.loop(2 * c, 2 * c + 2)
-        def _(p):
-            for i in range(2):
-                hop_up(blocks - 2 + i, p)
-                hop_down(1 - i, p)
-
+
+    def attend(c):
         rows = pl.ds(c * chunk, chunk)
         seen = (c + 1) * chunk
         keys[rows, :] = prepared(final[1, rows, :head], key_gain, rows).astype(BF16)
@@ -341,6 +362,29 @@
             out_ref[rows, j * head : (j + 1) * head] = jnp.dot(
                 probs, values[:seen, :], preferred_element_type=F32
             ).astype(BF16)
+
+    at_end = jnp.logical_or(z == 0, z == tensor_n - 1)
+
+    @pl.when(at_end)
+    def _():
+        behind = jnp.where(z == 0, down_lag, up_lag)
+        for c in range(chunks):
+            first = 0 if c == 0 else early + 4 * c + behind
+
+            @pl.loop(first, early + 4 * c + 4 + behind)
+            def _(n):
+                step(n)
+
+            attend(c)
+
+    @pl.when(jnp.logical_not(at_end))
+    def _():
+        @pl.loop(0, items + lag)
+        def _(n):
+            step(n)
+
+        for c in range(chunks):
+            attend(c)
 
     for i in range(1, plane_n):
         exchange(plane_sum, me, plane_peer(i)[1], plane_send.at[i], plane_recv).wait_send()

time: 200 us -> 101 us (0.51)
  Pallas kernels: 197 us -> 96.5 us
    pallas_call x1, Pallas kernels: 197 us -> 96.5 us  [shards(): pl.pallas_call(functools.partial(kernel, (group_n, dp_n, tensor_n, width)...]
where the time goes in v4:
time: 101 us; the launch traced here: 98.9 us
  Pallas kernels  96.5 us (96%)
  local copies, waits for them, and re-layouts  1.77 us (2%)
    pallas_call x1, Pallas kernels, shards(): pl.pallas_call(functools.partial(kernel, (group_n, dp_n, tensor_n, width)...  96.5 us

profile of v4, /device:TPU:2, one launch (start us, length us, event | category | flops | bytes accessed | tf_op | source)
XLA Modules:
  0.0 98.9 jit_solution(5981423440925859563)
XLA Ops:
  0.7 96.5 %step_and_prefill.1 = bf16[768,256]{1,0:T(8,128)(2,1)} custom-call(bf16[768,1280]{1,0:T(8,128)(2,1)} %act_hbm.1, f32[4,1,1280]{2,1,0:T(1,128)} %bitcast.11, f32[1920,128]{1,0:T(8,128)} %bitcast.7, bf16[3,640,128]{2,1,0:T(8,128)(2,1)} %bitcast.10, f32[1920,128]{1,0:T(8,128)} %bitcast.8, f32[1920,128]{1,0:T(8,128)} %bitcast.9, f32[2,128]{1,0:T(2,128)} %query_gain_ref.1, ...), custom_call_target="tpu_custom_call" | custom-call | tf_op jit(solution)/shard_map/step_and_prefill/pallas_call | solution.py:441
  97.2 1.8 %copy.14 = bf16[768,256]{1,0:T(8,128)(2,1)} copy(bf16[768,256]{1,0:T(8,128)(2,1)} %step_and_prefill.1) | data formatting | bytes 786432

commit v5 on v4

--- a/solution.py
+++ b/solution.py
@@ -45,12 +45,9 @@
     hubs = plane_n // tensor_n
     length, feat = act.shape
     slab_rows = grad.shape[1]
-    blocks = weights.shape[0] // 2
     head = 128
     chunk = 256 if length % 256 == 0 else length
     chunks = length // chunk
-    piece_rows = chunk // 2
-    pieces = length // piece_rows
 
     g = lax.axis_index("group")
     d = lax.axis_index("dp")
@@ -133,16 +130,9 @@
         variance_new = BETA_TWO * variance[rows, :] + (1.0 - BETA_TWO) * clipped * clipped
         return (master[rows, :] - step_size * moment_new / (jnp.sqrt(variance_new) + 1e-08)).astype(BF16)
 
-    def q_block(t):
-        return 3 * (t // 2) + 2 * (t % 2)
-
-    def kv_block(t):
-        return 3 * (t // 2) + 1
-
     def w_slot(r, t, part):
         rows = pl.ds(pl.multiple_of(r * slab_rows, 16), slab_rows)
-        column = 2 * q_block(t) + part if part < 2 else 2 * kv_block(t) + t % 2
-        return weights.at[column, rows, :]
+        return weights.at[3 * t + part, rows, :]
 
     owner, my_r = me // hubs, me % hubs
 
@@ -208,52 +198,56 @@
     def wait_send(copy):
         copy.wait_send()
 
-    def chain(buf, b, c, dev_z, ssem, rsem):
-        rows = pl.ds(pl.multiple_of(c * piece_rows, 16), piece_rows)
+    def chain(buf, column, c, dev_z, ssem, rsem):
+        rows = pl.ds(pl.multiple_of(c * chunk, 16), chunk)
         return pltpu.make_async_remote_copy(
-            src_ref=buf.at[b, rows, :], dst_ref=buf.at[b, rows, :], send_sem=ssem.at[b, c], recv_sem=rsem.at[b, c],
-            device_id=(g, d, dev_z), device_id_type=MESH,
+            src_ref=buf.at[column, rows, :], dst_ref=buf.at[column, rows, :], send_sem=ssem.at[column, c],
+            recv_sem=rsem.at[column, c], device_id=(g, d, dev_z), device_id_type=MESH,
         )
 
-    def chain_up(b, c):
-        return chain(up, b, c, jnp.minimum(z + 1, tensor_n - 1), up_send, up_recv)
-
-    def chain_down(b, c):
-        return chain(down, b, c, jnp.maximum(z - 1, 0), down_send, down_recv)
-
-    def span(b):
-        pair, j = b // 3, b % 3
-        return 2 * pair + j // 2, 2 * pair + (j + 1) // 2
-
-    def multiply(*todo):
+    def chain_up(column, c):
+        return chain(up, column, c, jnp.minimum(z + 1, tensor_n - 1), up_send, up_recv)
+
+    def chain_down(column, c):
+        return chain(down, column, c, jnp.maximum(z - 1, 0), down_send, down_recv)
+
+    def span(t, part):
+        first = t if part < 2 else 2 * (t // 2)
+        return first, first if part < 2 else first + 1
+
+    def multiply(t):
         @pl.loop(0, chunks)
         def _(c):
             rows = pl.ds(pl.multiple_of(c * chunk, 16), chunk)
-            for b in todo:
-                low, high = span(b)
-                both = jnp.concatenate([weights[2 * b], weights[2 * b + 1]], axis=1)
-                parts[b, rows, :] = jnp.dot(normed[rows, :], both, preferred_element_type=F32)
-
-                @pl.when(jnp.logical_and(z == 0, z < high))
-                def _():
-                    up[b, rows, :] = parts[b, rows, :].astype(BF16)
-                    for half in range(2):
-                        chain_up(b, 2 * c + half).start()
-
-                @pl.when(jnp.logical_and(z == tensor_n - 1, z > low))
-                def _():
-                    down[b, rows, :] = parts[b, rows, :].astype(BF16)
-                    for half in range(2):
-                        chain_down(b, 2 * c + half).start()
+            both = jnp.concatenate([weights[3 * t], weights[3 * t + 1]], axis=1)
+            product = jnp.dot(normed[rows, :], both, preferred_element_type=F32)
+            parts[3 * t, rows, :] = product[:, :head]
+            parts[3 * t + 1, rows, :] = product[:, head:]
+            parts[3 * t + 2, rows, :] = jnp.dot(normed[rows, :], weights[3 * t + 2], preferred_element_type=F32)
+
+            def begin(buf, copy, next_to):
+                for part in range(3):
+                    buf[3 * t + part, rows, :] = parts[3 * t + part, rows, :].astype(BF16)
+                    if part == 2:
+                        copy(3 * t + part, c).start()
+                    else:
+                        @pl.when(jnp.logical_and(t != z, t != next_to))
+                        def _():
+                            copy(3 * t + part, c).start()
+
+            @pl.when(z == 0)
+            def _():
+                begin(up, chain_up, 1)
+
+            @pl.when(z == tensor_n - 1)
+            def _():
+                begin(down, chain_down, tensor_n - 2)
 
     def slab(j):
         room = jnp.minimum(z, tensor_n - 1 - z)
         near = z + ((j + 1) // 2) * (2 * (j % 2) - 1)
         far = jnp.where(z < tensor_n - 1 - z, j, tensor_n - 1 - j)
         return jnp.where(j <= 2 * room, near, far)
-
-    def rank(t):
-        return jnp.where(t > z, 2 * (t - z) - 1, 2 * (z - t))
 
     def pass_on(t, i):
         r = (d + i) % hubs
@@ -275,64 +269,77 @@
         t = slab(j)
         for i in range(1, hubs):
             pass_on(t, i)
-        complete = rank(t + 1 - 2 * (t % 2)) < rank(t)
-
-        @pl.when(complete)
-        def _():
-            multiply(kv_block(t), q_block(t))
-
-        @pl.when(jnp.logical_not(complete))
-        def _():
-            multiply(q_block(t))
-
-    mine = (q_block(z), kv_block(z))
-    for slot in range(2):
-        final[slot] = parts[mine[slot]]
-
-    def hop(b, c, buf, copy, receives, sends):
-        low, high = span(b)
-        rows = pl.ds(pl.multiple_of(c * piece_rows, 16), piece_rows)
+        multiply(t)
+
+    @pl.when(z == 0)
+    def _():
+        for c in range(chunks):
+            for part in range(2):
+                chain_up(3 + part, c).start()
+
+    @pl.when(z == tensor_n - 1)
+    def _():
+        for c in range(chunks):
+            for part in range(2):
+                chain_down(3 * (tensor_n - 2) + part, c).start()
+
+    pair = 2 * (z // 2)
+    final[0] = parts[3 * z]
+    final[1] = parts[3 * z + 1]
+    final[2] = parts[3 * pair + 2]
+    final[3] = parts[3 * pair + 5]
+
+    def hop(t, part, c, buf, copy, receives, sends):
+        low, high = span(t, part)
+        rows = pl.ds(pl.multiple_of(c * chunk, 16), chunk)
+        column = 3 * t + part
 
         @pl.when(receives)
         def _():
-            copy(b, c).wait_recv()
-            arrived = buf[b, rows, :].astype(F32)
+            copy(column, c).wait_recv()
+            arrived = buf[column, rows, :].astype(F32)
 
             @pl.when(sends)
             def _():
-                buf[b, rows, :] = (parts[b, rows, :] + arrived).astype(BF16)
-                copy(b, c).start()
+                buf[column, rows, :] = (parts[column, rows, :] + arrived).astype(BF16)
+                copy(column, c).start()
 
             @pl.when(jnp.logical_and(low <= z, z <= high))
             def _():
-                slot = 1 - abs(b % 3 - 1)
+                slot = part if part < 2 else 2 + t % 2
                 final[slot, rows, :] += arrived
 
-    def hop_up(b, c):
-        high = span(b)[1]
-        hop(b, c, up, chain_up, jnp.logical_and(z > 0, z <= high), z < high)
-
-    def hop_down(b, c):
-        low = span(b)[0]
-        hop(b, c, down, chain_down, jnp.logical_and(z < tensor_n - 1, z >= low), z > low)
-
-    early = (blocks - 2) * pieces
-    items = blocks * pieces
-    lag = 3 * jnp.abs(tensor_n - 1 - 2 * z)
+    def hop_up(t, part, c):
+        high = span(t, part)[1]
+        hop(t, part, c, up, chain_up, jnp.logical_and(z > 0, z <= high), z < high)
+
+    def hop_down(t, part, c):
+        low = span(t, part)[0]
+        hop(t, part, c, down, chain_down, jnp.logical_and(z < tensor_n - 1, z >= low), z > low)
+
+    rounds = tensor_n * chunks
+    lag = jnp.abs(tensor_n - 1 - 2 * z)
     up_lag = jnp.where(2 * z < tensor_n, 0, lag)
     down_lag = lag - up_lag
 
-    def item(n):
-        late = n - early
-        b = jnp.where(late < 0, n // pieces, blocks - 2 + late % 2)
-        return b, jnp.where(late < 0, n % pieces, late // 2)
-
-    def step(n):
+    def turn(n):
         def one(n, hop_one, mirror):
-            @pl.when(jnp.logical_and(n >= 0, n < items))
+            slab_of = jnp.clip(n, 0, rounds - 1) // chunks
+            t = tensor_n - 1 - slab_of if mirror else slab_of
+            late = n >= rounds
+            c = jnp.where(late, n - rounds, n % chunks)
+            t = jnp.where(late, tensor_n - 2 if mirror else 1, t)
+
+            @pl.when(jnp.logical_and(n >= 0, n < rounds + chunks))
             def _():
-                b, c = item(jnp.clip(n, 0, items - 1))
-                hop_one(blocks - 1 - b if mirror else b, c)
+                @pl.when(jnp.logical_or(late, slab_of != 1))
+                def _():
+                    hop_one(t, 0, c)
+                    hop_one(t, 1, c)
+
+                @pl.when(jnp.logical_not(late))
+                def _():
+                    hop_one(t, 2, c)
 
         one(n - up_lag, hop_up, False)
         one(n - down_lag, hop_down, True)
@@ -347,13 +354,13 @@
     def attend(c):
         rows = pl.ds(c * chunk, chunk)
         seen = (c + 1) * chunk
-        keys[rows, :] = prepared(final[1, rows, :head], key_gain, rows).astype(BF16)
-        values[rows, :] = final[1, rows, head:].astype(BF16)
+        keys[rows, :] = prepared(final[2, rows, :], key_gain, rows).astype(BF16)
+        values[rows, :] = final[3, rows, :].astype(BF16)
         row_pos = lax.broadcasted_iota(jnp.int32, (chunk, seen), 0) + c * chunk
         col_pos = lax.broadcasted_iota(jnp.int32, (chunk, seen), 1)
         allowed = jnp.logical_and(col_pos <= row_pos, col_pos < live)
         for j in range(2):
-            raw = final[0, rows, j * head : (j + 1) * head]
+            raw = final[j, rows, :]
             query = (prepared(raw, query_gain_ref[j : j + 1, :], rows) * head ** (-0.5)).astype(BF16)
             scores = lax.dot_general(query, keys[:seen, :], (((1,), (1,)), ((), ())), preferred_element_type=F32)
             scores = jnp.where(allowed, scores, -1e30)
@@ -364,27 +371,19 @@
             ).astype(BF16)
 
     at_end = jnp.logical_or(z == 0, z == tensor_n - 1)
-
-    @pl.when(at_end)
-    def _():
-        behind = jnp.where(z == 0, down_lag, up_lag)
-        for c in range(chunks):
-            first = 0 if c == 0 else early + 4 * c + behind
-
-            @pl.loop(first, early + 4 * c + 4 + behind)
-            def _(n):
-                step(n)
-
-            attend(c)
-
-    @pl.when(jnp.logical_not(at_end))
-    def _():
-        @pl.loop(0, items + lag)
+    next_to = jnp.logical_or(z == 1, z == tensor_n - 2)
+
+    def stop(c):
+        end = rounds - chunks + c + 1 + lag
+        beside = rounds + jnp.maximum(c + 1, lag)
+        return jnp.where(at_end, end, jnp.where(next_to, beside, rounds + chunks + lag))
+
+    for c in range(chunks):
+        @pl.loop(0 if c == 0 else stop(c - 1), stop(c))
         def _(n):
-            step(n)
-
-        for c in range(chunks):
-            attend(c)
+            turn(n)
+
+        attend(c)
 
     for i in range(1, plane_n):
         exchange(plane_sum, me, plane_peer(i)[1], plane_send.at[i], plane_recv).wait_send()
@@ -404,19 +403,20 @@
             for part in range(3):
                 forwards(r, t, part, wait_send)
 
-    @pl.loop(0, blocks)
-    def _(b):
-        low, high = span(b)
-
-        @pl.loop(0, pieces)
-        def _(c):
-            @pl.when(z < high)
-            def _():
-                chain_up(b, c).wait_send()
-
-            @pl.when(z > low)
-            def _():
-                chain_down(b, c).wait_send()
+    @pl.loop(0, tensor_n)
+    def _(t):
+        for part in range(3):
+            low, high = span(t, part)
+
+            @pl.loop(0, chunks)
+            def _(c):
+                @pl.when(z < high)
+                def _():
+                    chain_up(3 * t + part, c).wait_send()
+
+                @pl.when(z > low)
+                def _():
+                    chain_down(3 * t + part, c).wait_send()
 
 
 def shards(sizes, activations, norm_gain, master_weight, grad, moment, variance, query_gain, key_gain, prompt_len):
@@ -427,9 +427,9 @@
     length, feat = activations.shape
     slab_rows, _, slots, head = master_weight.shape
     pair = 2 * head
-    blocks = 3 * tensor_n // 2
+    columns = 3 * tensor_n
     chunk = 256 if length % 256 == 0 else length
-    pieces = 2 * (length // chunk)
+    chunks = length // chunk
     cosine, sine = rope_tables(length, head)
 
     def flat(array):
@@ -451,11 +451,11 @@
             pltpu.VMEM((slab_rows * slots, head), F32),
             pltpu.VMEM((slab_rows * slots, head), F32),
             pltpu.VMEM((slots, slab_rows, head), BF16),
-            pltpu.VMEM((2 * blocks, feat, head), BF16),
-            pltpu.VMEM((blocks, length, pair), F32),
-            pltpu.VMEM((blocks, length, pair), BF16),
-            pltpu.VMEM((blocks, length, pair), BF16),
-            pltpu.VMEM((2, length, pair), F32),
+            pltpu.VMEM((columns, feat, head), BF16),
+            pltpu.VMEM((columns, length, head), F32),
+            pltpu.VMEM((columns, length, head), BF16),
+            pltpu.VMEM((columns, length, head), BF16),
+            pltpu.VMEM((4, length, head), F32),
             pltpu.VMEM((length, head), BF16),
             pltpu.VMEM((length, head), BF16),
             pltpu.VMEM((plane_n, 8, head), F32),
@@ -471,10 +471,10 @@
             dma((3,)),
             dma((hubs, tensor_n, 3)),
             dma((hubs, tensor_n, 3, group_n // 2 + dp_n - 1)),
-            dma((blocks, pieces)),
-            dma((blocks, pieces)),
-            dma((blocks, pieces)),
-            dma((blocks, pieces)),
+            dma((columns, chunks)),
+            dma((columns, chunks)),
+            dma((columns, chunks)),
+            dma((columns, chunks)),
         ],
         compiler_params=pltpu.CompilerParams(
             collective_id=0, has_side_effects=True, vmem_limit_bytes=60 * 1024 * 1024

time: 101 us -> 94.1 us (0.932); the launches traced: 98.9 us -> 94 us
  Pallas kernels: 96.5 us -> 91.5 us
    pallas_call x1, Pallas kernels: 96.5 us -> 91.5 us  [shards(): pl.pallas_call(functools.partial(kernel, (group_n, dp_n, tensor_n, width)...]
where the time goes in v5:
time: 94.1 us; the launch traced here: 94 us
  Pallas kernels  91.5 us (97%)
  local copies, waits for them, and re-layouts  1.77 us (2%)
    pallas_call x1, Pallas kernels, shards(): pl.pallas_call(functools.partial(kernel, (group_n, dp_n, tensor_n, width)...  91.5 us

profile of v5, /device:TPU:2, one launch (start us, length us, event | category | flops | bytes accessed | tf_op | source)
XLA Modules:
  0.0 94.0 jit_solution(7142593914098104781)
XLA Ops:
  0.7 91.5 %step_and_prefill.1 = bf16[768,256]{1,0:T(8,128)(2,1)} custom-call(bf16[768,1280]{1,0:T(8,128)(2,1)} %act_hbm.1, f32[4,1,1280]{2,1,0:T(1,128)} %bitcast.11, f32[1920,128]{1,0:T(8,128)} %bitcast.7, bf16[3,640,128]{2,1,0:T(8,128)(2,1)} %bitcast.10, f32[1920,128]{1,0:T(8,128)} %bitcast.8, f32[1920,128]{1,0:T(8,128)} %bitcast.9, f32[2,128]{1,0:T(2,128)} %query_gain_ref.1, ...), custom_call_target="tpu_custom_call" | custom-call | tf_op jit(solution)/shard_map/step_and_prefill/pallas_call | solution.py:441
  92.2 1.8 %copy.14 = bf16[768,256]{1,0:T(8,128)(2,1)} copy(bf16[768,256]{1,0:T(8,128)(2,1)} %step_and_prefill.1) | data formatting | bytes 786432

commit v6 on v5

--- a/solution.py
+++ b/solution.py
@@ -77,6 +77,10 @@
         pl.semaphore_signal(barrier, inc=1, device_id=plane_peer(i)[1], device_id_type=MESH)
     for i in range(1, tensor_n):
         pl.semaphore_signal(barrier, inc=1, device_id=line_peer(i)[1], device_id_type=MESH)
+    for h in range(1, chip_n):
+        for i in range(1, tensor_n):
+            beside = (((x + h) % chip_n) * 2 + core, d, (z + i) % tensor_n)
+            pl.semaphore_signal(barrier, inc=1, device_id=beside, device_id_type=MESH)
 
     loads[0].wait()
     tile = jnp.zeros((8, head), F32)
@@ -84,7 +88,7 @@
         piece = grad[s].astype(F32)
         tile += jnp.sum((piece * piece).reshape(slab_rows // 8, 8, head), axis=0)
     plane_sum[me] = tile
-    pl.semaphore_wait(barrier, plane_n + tensor_n - 2)
+    pl.semaphore_wait(barrier, plane_n - 1 + chip_n * (tensor_n - 1))
 
     def exchange(buf, slot, dev, ssem, rsem):
         return pltpu.make_async_remote_copy(
@@ -130,30 +134,34 @@
         variance_new = BETA_TWO * variance[rows, :] + (1.0 - BETA_TWO) * clipped * clipped
         return (master[rows, :] - step_size * moment_new / (jnp.sqrt(variance_new) + 1e-08)).astype(BF16)
 
-    def w_slot(r, t, part):
-        rows = pl.ds(pl.multiple_of(r * slab_rows, 16), slab_rows)
+    share = slab_rows // chip_n
+
+    def w_slot(r, h, t, part):
+        rows = pl.ds(pl.multiple_of(r * slab_rows + h * share, 16), share)
         return weights.at[3 * t + part, rows, :]
 
     owner, my_r = me // hubs, me % hubs
 
-    def to_hub(part):
+    def to_hub(h, part):
         return pltpu.make_async_remote_copy(
-            src_ref=own.at[part], dst_ref=w_slot(my_r, z, part), send_sem=hub_send.at[part],
-            recv_sem=w_recv.at[my_r, z, part], device_id=(g, d, owner), device_id_type=MESH,
+            src_ref=own.at[part, h * share : (h + 1) * share, :], dst_ref=w_slot(my_r, h, z, part),
+            send_sem=hub_send.at[h, part], recv_sem=w_recv.at[my_r * chip_n + h, z, part],
+            device_id=(((x + h) % chip_n) * 2 + core, d, owner), device_id_type=MESH,
         )
-
-    def place(part):
-        @pl.when(z == owner)
-        def _():
-            w_slot(my_r, z, part)[...] = own[part]
-
-        @pl.when(z != owner)
-        def _():
-            to_hub(part).start()
 
     for part in range(3):
         own[part] = updated(part)
-        place(part)
+
+        @pl.when(z == owner)
+        def _():
+            w_slot(my_r, 0, z, part)[...] = own[part, :share]
+
+        @pl.when(z != owner)
+        def _():
+            to_hub(0, part).start()
+
+        for h in range(1, chip_n):
+            to_hub(h, part).start()
 
     square = row_sum[z]
     for i in range(1, tensor_n):
@@ -166,31 +174,35 @@
         scale = jnp.broadcast_to(scale_row[:, c * chunk : (c + 1) * chunk], (head, chunk)).T[:, :1]
         normed[rows, :] = (act[rows, :].astype(F32) * scale * gain_ref[z]).astype(BF16)
 
-    def forward(r, t, part, slot, dev):
+    def forward(r, h, t, part, slot, dev):
         return pltpu.make_async_remote_copy(
-            src_ref=w_slot(r, t, part), dst_ref=w_slot(r, t, part), send_sem=w_send.at[r, t, part, slot],
-            recv_sem=w_recv.at[r, t, part], device_id=dev, device_id_type=MESH,
+            src_ref=w_slot(r, h, t, part), dst_ref=w_slot(r, h, t, part),
+            send_sem=w_send.at[r * chip_n + h, t, part, slot], recv_sem=w_recv.at[r * chip_n + h, t, part],
+            device_id=dev, device_id_type=MESH,
         )
 
-    def forwards(r, t, part, act_on):
-        hub = z * hubs + r
-        hub_g, hub_d = hub // dp_n, hub % dp_n
-        same_core = core == hub_g % 2
-        at_hub = hub == me
-
-        @pl.when(at_hub)
+    def origin(r):
+        hub_g = (z * hubs + r) // dp_n
+        return hub_g // 2, hub_g % 2, (z * hubs + r) % dp_n
+
+    def forwards(r, h, t, part, act_on):
+        from_x, from_core, from_d = origin(r)
+        same_core = core == from_core
+        same_line = jnp.logical_and(same_core, d == from_d)
+
+        @pl.when(jnp.logical_and(same_line, x == (from_x + h) % chip_n))
         def _():
             for i in range(1, chip_n):
-                act_on(forward(r, t, part, i - 1, (((x + i) % chip_n) * 2 + core, d, z)))
-
-        @pl.when(jnp.logical_and(same_core, d == hub_d))
+                act_on(forward(r, h, t, part, i - 1, (((x + i) % chip_n) * 2 + core, d, z)))
+
+        @pl.when(same_line)
         def _():
             for i in range(1, dp_n):
-                act_on(forward(r, t, part, chip_n - 2 + i, (g, (d + i) % dp_n, z)))
+                act_on(forward(r, h, t, part, chip_n - 2 + i, (g, (d + i) % dp_n, z)))
 
         @pl.when(same_core)
         def _():
-            act_on(forward(r, t, part, chip_n + dp_n - 2, (x * 2 + 1 - core, d, z)))
+            act_on(forward(r, h, t, part, chip_n + dp_n - 2, (x * 2 + 1 - core, d, z)))
 
     def start(copy):
         copy.start()
@@ -249,27 +261,35 @@
         far = jnp.where(z < tensor_n - 1 - z, j, tensor_n - 1 - j)
         return jnp.where(j <= 2 * room, near, far)
 
-    def pass_on(t, i):
+    def pass_on(t, i, q):
         r = (d + i) % hubs
+        h = (x - origin(r)[0] + chip_n + q) % chip_n
         for part in range(3):
-            @pl.when(jnp.logical_not(jnp.logical_and(z * hubs + r == me, t == z)))
+            @pl.when(jnp.logical_not(jnp.logical_and(z * hubs + r == me, jnp.logical_and(t == z, h == 0))))
             def _():
-                forward(r, t, part, 0, (g, d, z)).wait_recv()
-
-            forwards(r, t, part, start)
-
-    pass_on(slab(0), 0)
-
-    @pl.loop(0, tensor_n)
+                forward(r, h, t, part, 0, (g, d, z)).wait_recv()
+
+            forwards(r, h, t, part, start)
+
+    @pl.loop(-2, tensor_n)
     def _(j):
-        @pl.when(j + 1 < tensor_n)
-        def _():
-            pass_on(slab(jnp.minimum(j + 1, tensor_n - 1)), 0)
-
-        t = slab(j)
-        for i in range(1, hubs):
-            pass_on(t, i)
-        multiply(t)
+        @pl.when(j + 2 < tensor_n)
+        def _():
+            pass_on(slab(jnp.minimum(j + 2, tensor_n - 1)), 0, 0)
+
+        @pl.when(jnp.logical_and(j + 1 >= 0, j + 1 < tensor_n))
+        def _():
+            t = slab(jnp.clip(j + 1, 0, tensor_n - 1))
+            for q in range(1, chip_n):
+                pass_on(t, 0, q)
+
+        @pl.when(j >= 0)
+        def _():
+            t = slab(jnp.maximum(j, 0))
+            for i in range(1, hubs):
+                for q in range(chip_n):
+                    pass_on(t, i, q)
+            multiply(t)
 
     @pl.when(z == 0)
     def _():
@@ -392,16 +412,20 @@
         exchange(line_sum, z, dev, line_send.at[i], line_recv).wait_send()
         exchange(row_sum, z, dev, row_send.at[i], row_recv).wait_send()
 
-    @pl.when(z != owner)
-    def _():
-        for part in range(3):
-            to_hub(part).wait_send()
+    for part in range(3):
+        for h in range(1, chip_n):
+            to_hub(h, part).wait_send()
+
+        @pl.when(z != owner)
+        def _():
+            to_hub(0, part).wait_send()
 
     @pl.loop(0, tensor_n)
     def _(t):
         for r in range(hubs):
-            for part in range(3):
-                forwards(r, t, part, wait_send)
+            for h in range(chip_n):
+                for part in range(3):
+                    forwards(r, h, t, part, wait_send)
 
     @pl.loop(0, tensor_n)
     def _(t):
@@ -427,6 +451,7 @@
     length, feat = activations.shape
     slab_rows, _, slots, head = master_weight.shape
     pair = 2 * head
+    chip_n = group_n // 2
     columns = 3 * tensor_n
     chunk = 256 if length % 256 == 0 else length
     chunks = length // chunk
@@ -468,9 +493,9 @@
             dma((tensor_n,)),
             dma((tensor_n,)),
             dma((tensor_n,)),
-            dma((3,)),
-            dma((hubs, tensor_n, 3)),
-            dma((hubs, tensor_n, 3, group_n // 2 + dp_n - 1)),
+            dma((chip_n, 3)),
+            dma((hubs * chip_n, tensor_n, 3)),
+            dma((hubs * chip_n, tensor_n, 3, chip_n + dp_n - 1)),
             dma((columns, chunks)),
             dma((columns, chunks)),
             dma((columns, chunks)),

time: 94.1 us -> 96.3 us (1.023)
  Pallas kernels: 91.5 us -> 93.4 us
    pallas_call x1, Pallas kernels: 91.5 us -> 93.4 us  [shards(): pl.pallas_call(functools.partial(kernel, (group_n, dp_n, tensor_n, width)...]
where the time goes in v6:
time: 96.3 us; the launch traced here: 95.9 us
  Pallas kernels  93.4 us (97%)
  local copies, waits for them, and re-layouts  1.77 us (2%)
    pallas_call x1, Pallas kernels, shards(): pl.pallas_call(functools.partial(kernel, (group_n, dp_n, tensor_n, width)...  93.4 us

profile of v6, /device:TPU:2, one launch (start us, length us, event | category | flops | bytes accessed | tf_op | source)
XLA Modules:
  0.0 95.9 jit_solution(8436482177013865920)
XLA Ops:
  0.7 93.4 %step_and_prefill.1 = bf16[768,256]{1,0:T(8,128)(2,1)} custom-call(bf16[768,1280]{1,0:T(8,128)(2,1)} %act_hbm.1, f32[4,1,1280]{2,1,0:T(1,128)} %bitcast.11, f32[1920,128]{1,0:T(8,128)} %bitcast.7, bf16[3,640,128]{2,1,0:T(8,128)(2,1)} %bitcast.10, f32[1920,128]{1,0:T(8,128)} %bitcast.8, f32[1920,128]{1,0:T(8,128)} %bitcast.9, f32[2,128]{1,0:T(2,128)} %query_gain_ref.1, ...), custom_call_target="tpu_custom_call" | custom-call | tf_op jit(solution)/shard_map/step_and_prefill/pallas_call | solution.py:466
  94.1 1.8 %copy.14 = bf16[768,256]{1,0:T(8,128)(2,1)} copy(bf16[768,256]{1,0:T(8,128)(2,1)} %step_and_prefill.1) | data formatting | bytes 786432

commit v7 on v5

--- a/solution.py
+++ b/solution.py
@@ -112,49 +112,6 @@
     line_sum[z] = total
     for i in range(1, tensor_n):
         exchange(line_sum, z, line_peer(i)[1], line_send.at[i], line_recv).start()
-    for load in loads[2:]:
-        load.wait()
-    for i in range(1, tensor_n):
-        t, dev = line_peer(i)
-        exchange(line_sum, t, dev, line_send.at[i], line_recv).wait_recv()
-        total += line_sum[t]
-    sumsq = jnp.sum(jnp.sum(total, axis=0, keepdims=True), axis=1, keepdims=True)
-    clip = 1.0 / jnp.sqrt(sumsq + 1e-12)
-
-    step_size = STEP_SCALE * width ** (-0.5)
-
-    def updated(s):
-        clipped = grad[s].astype(F32) * clip
-        rows = pl.ds(s, slab_rows, stride=3)
-        moment_new = BETA_ONE * moment[rows, :] + (1.0 - BETA_ONE) * clipped
-        variance_new = BETA_TWO * variance[rows, :] + (1.0 - BETA_TWO) * clipped * clipped
-        return (master[rows, :] - step_size * moment_new / (jnp.sqrt(variance_new) + 1e-08)).astype(BF16)
-
-    def w_slot(r, t, part):
-        rows = pl.ds(pl.multiple_of(r * slab_rows, 16), slab_rows)
-        return weights.at[3 * t + part, rows, :]
-
-    owner, my_r = me // hubs, me % hubs
-
-    def to_hub(part):
-        return pltpu.make_async_remote_copy(
-            src_ref=own.at[part], dst_ref=w_slot(my_r, z, part), send_sem=hub_send.at[part],
-            recv_sem=w_recv.at[my_r, z, part], device_id=(g, d, owner), device_id_type=MESH,
-        )
-
-    def place(part):
-        @pl.when(z == owner)
-        def _():
-            w_slot(my_r, z, part)[...] = own[part]
-
-        @pl.when(z != owner)
-        def _():
-            to_hub(part).start()
-
-    for part in range(3):
-        own[part] = updated(part)
-        place(part)
-
     square = row_sum[z]
     for i in range(1, tensor_n):
         t, dev = line_peer(i)
@@ -166,6 +123,49 @@
         scale = jnp.broadcast_to(scale_row[:, c * chunk : (c + 1) * chunk], (head, chunk)).T[:, :1]
         normed[rows, :] = (act[rows, :].astype(F32) * scale * gain_ref[z]).astype(BF16)
 
+    for load in loads[2:]:
+        load.wait()
+    for i in range(1, tensor_n):
+        t, dev = line_peer(i)
+        exchange(line_sum, t, dev, line_send.at[i], line_recv).wait_recv()
+        total += line_sum[t]
+    sumsq = jnp.sum(jnp.sum(total, axis=0, keepdims=True), axis=1, keepdims=True)
+    clip = 1.0 / jnp.sqrt(sumsq + 1e-12)
+
+    step_size = STEP_SCALE * width ** (-0.5)
+
+    def updated(s):
+        clipped = grad[s].astype(F32) * clip
+        rows = pl.ds(s, slab_rows, stride=3)
+        moment_new = BETA_ONE * moment[rows, :] + (1.0 - BETA_ONE) * clipped
+        variance_new = BETA_TWO * variance[rows, :] + (1.0 - BETA_TWO) * clipped * clipped
+        return (master[rows, :] - step_size * moment_new / (jnp.sqrt(variance_new) + 1e-08)).astype(BF16)
+
+    def w_slot(r, t, part):
+        rows = pl.ds(pl.multiple_of(r * slab_rows, 16), slab_rows)
+        return weights.at[3 * t + part, rows, :]
+
+    owner, my_r = me // hubs, me % hubs
+
+    def to_hub(part):
+        return pltpu.make_async_remote_copy(
+            src_ref=own.at[part], dst_ref=w_slot(my_r, z, part), send_sem=hub_send.at[part],
+            recv_sem=w_recv.at[my_r, z, part], device_id=(g, d, owner), device_id_type=MESH,
+        )
+
+    def place(part):
+        @pl.when(z == owner)
+        def _():
+            w_slot(my_r, z, part)[...] = own[part]
+
+        @pl.when(z != owner)
+        def _():
+            to_hub(part).start()
+
+    for part in (2, 0, 1):
+        own[part] = updated(part)
+        place(part)
+
     def forward(r, t, part, slot, dev):
         return pltpu.make_async_remote_copy(
             src_ref=w_slot(r, t, part), dst_ref=w_slot(r, t, part), send_sem=w_send.at[r, t, part, slot],
@@ -215,18 +215,17 @@
         first = t if part < 2 else 2 * (t // 2)
         return first, first if part < 2 else first + 1
 
-    def multiply(t):
+    def multiply(t, todo):
         @pl.loop(0, chunks)
         def _(c):
             rows = pl.ds(pl.multiple_of(c * chunk, 16), chunk)
-            both = jnp.concatenate([weights[3 * t], weights[3 * t + 1]], axis=1)
-            product = jnp.dot(normed[rows, :], both, preferred_element_type=F32)
-            parts[3 * t, rows, :] = product[:, :head]
-            parts[3 * t + 1, rows, :] = product[:, head:]
-            parts[3 * t + 2, rows, :] = jnp.dot(normed[rows, :], weights[3 * t + 2], preferred_element_type=F32)
+            some = jnp.concatenate([weights[3 * t + part] for part in todo], axis=1)
+            product = jnp.dot(normed[rows, :], some, preferred_element_type=F32)
+            for i, part in enumerate(todo):
+                parts[3 * t + part, rows, :] = product[:, i * head : (i + 1) * head]
 
             def begin(buf, copy, next_to):
-                for part in range(3):
+                for part in todo:
                     buf[3 * t + part, rows, :] = parts[3 * t + part, rows, :].astype(BF16)
                     if part == 2:
                         copy(3 * t + part, c).start()
@@ -249,27 +248,31 @@
         far = jnp.where(z < tensor_n - 1 - z, j, tensor_n - 1 - j)
         return jnp.where(j <= 2 * room, near, far)
 
-    def pass_on(t, i):
+    def pass_on(t, i, todo):
         r = (d + i) % hubs
-        for part in range(3):
+        for part in todo:
             @pl.when(jnp.logical_not(jnp.logical_and(z * hubs + r == me, t == z)))
             def _():
                 forward(r, t, part, 0, (g, d, z)).wait_recv()
 
             forwards(r, t, part, start)
 
-    pass_on(slab(0), 0)
+    pass_on(slab(0), 0, (2, 0, 1))
 
     @pl.loop(0, tensor_n)
     def _(j):
-        @pl.when(j + 1 < tensor_n)
-        def _():
-            pass_on(slab(jnp.minimum(j + 1, tensor_n - 1)), 0)
-
         t = slab(j)
         for i in range(1, hubs):
-            pass_on(t, i)
-        multiply(t)
+            pass_on(t, i, (2,))
+        multiply(t, (2,))
+
+        @pl.when(j + 1 < tensor_n)
+        def _():
+            pass_on(slab(jnp.minimum(j + 1, tensor_n - 1)), 0, (2, 0, 1))
+
+        for i in range(1, hubs):
+            pass_on(t, i, (0, 1))
+        multiply(t, (0, 1))
 
     @pl.when(z == 0)
     def _():
@@ -317,29 +320,33 @@
         low = span(t, part)[0]
         hop(t, part, c, down, chain_down, jnp.logical_and(z < tensor_n - 1, z >= low), z > low)
 
-    rounds = tensor_n * chunks
+    per_slab = chunks + 1
+    rounds = tensor_n * per_slab
     lag = jnp.abs(tensor_n - 1 - 2 * z)
     up_lag = jnp.where(2 * z < tensor_n, 0, lag)
     down_lag = lag - up_lag
 
     def turn(n):
         def one(n, hop_one, mirror):
-            slab_of = jnp.clip(n, 0, rounds - 1) // chunks
+            slab_of = jnp.clip(n, 0, rounds - 1) // per_slab
             t = tensor_n - 1 - slab_of if mirror else slab_of
             late = n >= rounds
-            c = jnp.where(late, n - rounds, n % chunks)
+            place = jnp.clip(n, 0, rounds - 1) % per_slab
+            c = jnp.where(late, n - rounds, jnp.maximum(place - 1, 0))
             t = jnp.where(late, tensor_n - 2 if mirror else 1, t)
+            whole = jnp.logical_and(jnp.logical_not(late), place == 0)
 
             @pl.when(jnp.logical_and(n >= 0, n < rounds + chunks))
             def _():
-                @pl.when(jnp.logical_or(late, slab_of != 1))
+                @pl.when(whole)
+                def _():
+                    for i in range(chunks):
+                        hop_one(t, 2, i)
+
+                @pl.when(jnp.logical_and(jnp.logical_not(whole), jnp.logical_or(late, slab_of != 1)))
                 def _():
                     hop_one(t, 0, c)
                     hop_one(t, 1, c)
-
-                @pl.when(jnp.logical_not(late))
-                def _():
-                    hop_one(t, 2, c)
 
         one(n - up_lag, hop_up, False)
         one(n - down_lag, hop_down, True)

time: 94.1 us -> 95.6 us (1.016)
  Pallas kernels: 91.5 us -> 93 us
    pallas_call x1, Pallas kernels: 91.5 us -> 93 us  [shards(): pl.pallas_call(functools.partial(kernel, (group_n, dp_n, tensor_n, width)...]
where the time goes in v7:
time: 95.6 us; the launch traced here: 95.4 us
  Pallas kernels  93 us (97%)
  local copies, waits for them, and re-layouts  1.77 us (2%)
    pallas_call x1, Pallas kernels, shards(): pl.pallas_call(functools.partial(kernel, (group_n, dp_n, tensor_n, width)...  93 us

profile of v7, /device:TPU:2, one launch (start us, length us, event | category | flops | bytes accessed | tf_op | source)
XLA Modules:
  0.0 95.4 jit_solution(10981122434724102696)
XLA Ops:
  0.7 93.0 %step_and_prefill.1 = bf16[768,256]{1,0:T(8,128)(2,1)} custom-call(bf16[768,1280]{1,0:T(8,128)(2,1)} %act_hbm.1, f32[4,1,1280]{2,1,0:T(1,128)} %bitcast.11, f32[1920,128]{1,0:T(8,128)} %bitcast.7, bf16[3,640,128]{2,1,0:T(8,128)(2,1)} %bitcast.10, f32[1920,128]{1,0:T(8,128)} %bitcast.8, f32[1920,128]{1,0:T(8,128)} %bitcast.9, f32[2,128]{1,0:T(2,128)} %query_gain_ref.1, ...), custom_call_target="tpu_custom_call" | custom-call | tf_op jit(solution)/shard_map/step_and_prefill/pallas_call | solution.py:448
  93.7 1.8 %copy.14 = bf16[768,256]{1,0:T(8,128)(2,1)} copy(bf16[768,256]{1,0:T(8,128)(2,1)} %step_and_prefill.1) | data formatting | bytes 786432

commit v8 on v5

--- a/solution.py
+++ b/solution.py
@@ -112,49 +112,6 @@
     line_sum[z] = total
     for i in range(1, tensor_n):
         exchange(line_sum, z, line_peer(i)[1], line_send.at[i], line_recv).start()
-    for load in loads[2:]:
-        load.wait()
-    for i in range(1, tensor_n):
-        t, dev = line_peer(i)
-        exchange(line_sum, t, dev, line_send.at[i], line_recv).wait_recv()
-        total += line_sum[t]
-    sumsq = jnp.sum(jnp.sum(total, axis=0, keepdims=True), axis=1, keepdims=True)
-    clip = 1.0 / jnp.sqrt(sumsq + 1e-12)
-
-    step_size = STEP_SCALE * width ** (-0.5)
-
-    def updated(s):
-        clipped = grad[s].astype(F32) * clip
-        rows = pl.ds(s, slab_rows, stride=3)
-        moment_new = BETA_ONE * moment[rows, :] + (1.0 - BETA_ONE) * clipped
-        variance_new = BETA_TWO * variance[rows, :] + (1.0 - BETA_TWO) * clipped * clipped
-        return (master[rows, :] - step_size * moment_new / (jnp.sqrt(variance_new) + 1e-08)).astype(BF16)
-
-    def w_slot(r, t, part):
-        rows = pl.ds(pl.multiple_of(r * slab_rows, 16), slab_rows)
-        return weights.at[3 * t + part, rows, :]
-
-    owner, my_r = me // hubs, me % hubs
-
-    def to_hub(part):
-        return pltpu.make_async_remote_copy(
-            src_ref=own.at[part], dst_ref=w_slot(my_r, z, part), send_sem=hub_send.at[part],
-            recv_sem=w_recv.at[my_r, z, part], device_id=(g, d, owner), device_id_type=MESH,
-        )
-
-    def place(part):
-        @pl.when(z == owner)
-        def _():
-            w_slot(my_r, z, part)[...] = own[part]
-
-        @pl.when(z != owner)
-        def _():
-            to_hub(part).start()
-
-    for part in range(3):
-        own[part] = updated(part)
-        place(part)
-
     square = row_sum[z]
     for i in range(1, tensor_n):
         t, dev = line_peer(i)
@@ -165,6 +122,49 @@
         rows = pl.ds(c * chunk, chunk)
         scale = jnp.broadcast_to(scale_row[:, c * chunk : (c + 1) * chunk], (head, chunk)).T[:, :1]
         normed[rows, :] = (act[rows, :].astype(F32) * scale * gain_ref[z]).astype(BF16)
+
+    for load in loads[2:]:
+        load.wait()
+    for i in range(1, tensor_n):
+        t, dev = line_peer(i)
+        exchange(line_sum, t, dev, line_send.at[i], line_recv).wait_recv()
+        total += line_sum[t]
+    sumsq = jnp.sum(jnp.sum(total, axis=0, keepdims=True), axis=1, keepdims=True)
+    clip = 1.0 / jnp.sqrt(sumsq + 1e-12)
+
+    step_size = STEP_SCALE * width ** (-0.5)
+
+    def updated(s):
+        clipped = grad[s].astype(F32) * clip
+        rows = pl.ds(s, slab_rows, stride=3)
+        moment_new = BETA_ONE * moment[rows, :] + (1.0 - BETA_ONE) * clipped
+        variance_new = BETA_TWO * variance[rows, :] + (1.0 - BETA_TWO) * clipped * clipped
+        return (master[rows, :] - step_size * moment_new / (jnp.sqrt(variance_new) + 1e-08)).astype(BF16)
+
+    def w_slot(r, t, part):
+        rows = pl.ds(pl.multiple_of(r * slab_rows, 16), slab_rows)
+        return weights.at[3 * t + part, rows, :]
+
+    owner, my_r = me // hubs, me % hubs
+
+    def to_hub(part):
+        return pltpu.make_async_remote_copy(
+            src_ref=own.at[part], dst_ref=w_slot(my_r, z, part), send_sem=hub_send.at[part],
+            recv_sem=w_recv.at[my_r, z, part], device_id=(g, d, owner), device_id_type=MESH,
+        )
+
+    def place(part):
+        @pl.when(z == owner)
+        def _():
+            w_slot(my_r, z, part)[...] = own[part]
+
+        @pl.when(z != owner)
+        def _():
+            to_hub(part).start()
+
+    for part in range(3):
+        own[part] = updated(part)
+        place(part)
 
     def forward(r, t, part, slot, dev):
         return pltpu.make_async_remote_copy(

time: 94.1 us -> 94.1 us (level)
  no operation moved by 1% of the time
where the time goes in v8:
time: 94.1 us; the launch traced here: 94 us
  Pallas kernels  91.5 us (97%)
  local copies, waits for them, and re-layouts  1.77 us (2%)
    pallas_call x1, Pallas kernels, shards(): pl.pallas_call(functools.partial(kernel, (group_n, dp_n, tensor_n, width)...  91.5 us

profile of v8, /device:TPU:2, one launch (start us, length us, event | category | flops | bytes accessed | tf_op | source)
XLA Modules:
  0.0 94.0 jit_solution(16842294159678843819)
XLA Ops:
  0.7 91.5 %step_and_prefill.1 = bf16[768,256]{1,0:T(8,128)(2,1)} custom-call(bf16[768,1280]{1,0:T(8,128)(2,1)} %act_hbm.1, f32[4,1,1280]{2,1,0:T(1,128)} %bitcast.11, f32[1920,128]{1,0:T(8,128)} %bitcast.7, bf16[3,640,128]{2,1,0:T(8,128)(2,1)} %bitcast.10, f32[1920,128]{1,0:T(8,128)} %bitcast.8, f32[1920,128]{1,0:T(8,128)} %bitcast.9, f32[2,128]{1,0:T(2,128)} %query_gain_ref.1, ...), custom_call_target="tpu_custom_call" | custom-call | tf_op jit(solution)/shard_map/step_and_prefill/pallas_call | solution.py:441
  92.2 1.8 %copy.14 = bf16[768,256]{1,0:T(8,128)(2,1)} copy(bf16[768,256]{1,0:T(8,128)(2,1)} %step_and_prefill.1) | data formatting | bytes 786432
